TPU v7x, 256 devices: a whole 4x4x8 slice. The times are simulated.
256 devices in a mesh: docs: 128 (over z, x, y), tiles: 2 (over core).
Axes of the slice: x: 4, y: 4, z: 8, core: 2. Of those that a mesh axis runs over, the one named last changes fastest.
Arguments:
- embeddings: float32 [32768, 1024], P(('docs', 'tiles')), may hold values from -6 to 6
- cluster_of: int32 [32768], P(('docs', 'tiles')), may hold values from 0 to 255, as said below
- row_lists: int32 [256, 512], P('docs'), may hold values from -1 to 511, as said below
- row_counts: int32 [256], P('docs'), may hold values from 0 to 512, as said below
Outputs:
- max_cosine: float32 [32768], P(('docs', 'tiles'))
Inputs may be any that keep to these rules, and one draw needn't show every extreme that they name: `cluster_of`: clusters 2 * d to 2 * d + 1 have home d. The documents of one device have at most 2 of one home, and 16 homes receive exactly 2 from every device. `row_lists`: row c lists the places of cluster c's documents in their earlier order and holds -1 from position row_counts[c] on. `row_counts`: some cluster holds 512 documents.
All inputs are finite; a program needn't handle non-finite values.
Results may differ from a plain program's by a relative error of at most 0.0003.
Values sent between devices are 32-bit elements; how exact they have to be, the bound alone decides.
No kernel may reach another device: no remote copies, remote signals or barrier semaphores. Data moves between devices by JAX's collectives and lax.ppermute only.
A program may use at most 64 MiB of HBM per device.

v0:
```python
import jax
import jax.numpy as jnp
from jax import lax
from jax.sharding import PartitionSpec as P

TILE = 256


EPS = 1e-06


def tile_rows(flat_rows, safe_lists, start_row, tile_size):
    return flat_rows[lax.dynamic_slice_in_dim(safe_lists, start_row, tile_size, 0)]


def row_block(flat_rows, safe_lists, maxima, row_tile, first_block, stride, tile_size):
    query_rows = tile_rows(flat_rows, safe_lists, row_tile * tile_size, tile_size)
    query_pos = row_tile * tile_size + jnp.arange(tile_size, dtype=jnp.int32)
    steps_count = (row_tile + 1 - first_block + stride - 1) // stride

    def inner_step(step_index, best_score):
        col_tile = first_block + step_index * stride
        key_rows = tile_rows(flat_rows, safe_lists, col_tile * tile_size, tile_size)
        scores = jnp.einsum(
            "qd,kd->qk",
            query_rows,
            key_rows,
            precision=lax.Precision.HIGHEST,
            preferred_element_type=jnp.float32,
        )
        key_pos = col_tile * tile_size + jnp.arange(tile_size, dtype=jnp.int32)
        masked = jnp.where(key_pos[None, :] < query_pos[:, None], scores, -1.0)
        return jnp.maximum(best_score, jnp.max(masked, axis=1))

    best_score = lax.fori_loop(
        0, steps_count, inner_step, jnp.full((tile_size,), -1.0, jnp.float32)
    )
    return lax.dynamic_update_slice_in_dim(maxima, best_score, row_tile * tile_size, 0)


def local(embeddings, cluster_of, row_lists, row_counts):
    n_docs = lax.axis_size("docs")
    n_tiles = lax.axis_size("tiles")
    doc_count = embeddings.shape[0]
    feat_width = embeddings.shape[1]
    send_cap = n_tiles * doc_count // n_docs
    cl_local = row_lists.shape[0]
    cap_rows = row_lists.shape[1]
    tile_size = TILE
    core_index = lax.axis_index("tiles")
    home_index = cluster_of // cl_local
    same_home = home_index[:, None] == home_index[None, :]
    earlier = (
        jnp.arange(doc_count, dtype=jnp.int32)[:, None]
        > jnp.arange(doc_count, dtype=jnp.int32)[None, :]
    )
    slot_rank = jnp.sum((same_home & earlier).astype(jnp.int32), axis=1)
    unit_rows = embeddings * lax.rsqrt(
        jnp.sum(embeddings * embeddings, axis=1, keepdims=True) + EPS
    )
    outgoing = (
        jnp.zeros((n_docs, send_cap, feat_width), jnp.float32)
        .at[home_index, slot_rank]
        .set(unit_rows)
    )
    received = lax.all_to_all(outgoing, "docs", split_axis=0, concat_axis=0, tiled=True)
    buffer = lax.all_gather(received[None], "tiles", axis=0, tiled=True)
    flat_rows = buffer.reshape(-1, feat_width)
    buffer_rows = flat_rows.shape[0]
    place_max = jnp.full((buffer_rows,), -1.0, jnp.float32)
    for cluster_local in range(cl_local):
        list_row = row_lists[cluster_local]
        list_count = row_counts[cluster_local]
        safe_lists = jnp.maximum(list_row, 0)
        tile_count = (list_count + tile_size - 1) // tile_size
        maxima = jnp.full((cap_rows,), -1.0, jnp.float32)
        half_tiles = (tile_count + 1) // 2
        row_start = jnp.where(core_index == 0, 0, half_tiles)
        row_stop = jnp.where(core_index == 0, half_tiles, tile_count)

        def outer_step(row_tile, current):
            return row_block(flat_rows, safe_lists, current, row_tile, 0, 1, tile_size)

        maxima = lax.fori_loop(row_start, row_stop, outer_step, maxima)
        target = jnp.where(
            jnp.arange(cap_rows, dtype=jnp.int32) < list_count, list_row, buffer_rows
        )
        place_max = place_max.at[target].set(maxima, mode="drop")
    merged = lax.pmax(place_max, "tiles")
    own_half = lax.dynamic_index_in_dim(
        merged.reshape(n_tiles, n_docs, send_cap), core_index, 0, keepdims=False
    )
    returned = lax.all_to_all(own_half, "docs", split_axis=0, concat_axis=0, tiled=True)
    return returned[home_index, slot_rank]


def solution(mesh):
    placed = (P(("docs", "tiles"), None), P(("docs", "tiles")), P("docs", None), P("docs"))
    return jax.shard_map(
        local, mesh=mesh, in_specs=placed, out_specs=P(("docs", "tiles")), check_vma=False
    )
```

profile of v0, /device:TPU:1, one launch (start us, length us, event | category | flops | bytes accessed | tf_op | source)
XLA Modules:
  0.0 132.8 jit_solution(4568780380886305893)
XLA Ops:
  6.5 0.0 all-gather.3.cloned.1.call-start
  6.5 0.7 and_select_fusion
  7.2 0.2 convert_reduce_fusion
  7.4 1.3 fusion.14
  8.6 1.2 multiply_reduce_fusion
  9.8 1.1 broadcast_multiply_fusion
  11.0 0.3 broadcast_in_dim.62
  11.2 7.5 %scatter_fusion = f32[128,2,1024]{2,1,0:T(2,128)S(1)} fusion(f32[128,2,1024]{2,1,0:T(2,128)S(1)} %broadcast_in_dim.62, s32[128]{0:T(128)S(1)} %get-tuple-element.444, f32[128,1024]{1,0:T(8,128)S(1)} %broadcast_multiply_fusion), kind=kCustom, calls=%fused_computation.5 | custom fusion | bytes 1573888 | tf_op jit(solution)/shard_map/scatter | solution.py:64
  18.7 0.0 copy-start.3
  18.8 0.0 copy-start.1
  18.8 44.9 %all_to_all.17 = f32[128,2,1024]{2,1,0:T(2,128)} all-to-all(f32[128,2,1024]{2,1,0:T(2,128)S(1)} %scatter_fusion), channel_id=1, replica_groups=mesh['docs'=128,'tiles'=2] {'docs'}, dimensions={0} | all-to-all | bytes 2097152 | tf_op jit(solution)/shard_map/all_to_all | solution.py:66
  63.6 0.0 all-gather.3.cloned.1.call-update
  63.6 0.0 copy-done.3
  63.7 0.6 fusion.15
  65.5 0.0 copy-done.1
  65.6 1.8 %compare_select_fusion.4 = (s32[512,1]{0,1:T(1,128)}, s32[512,1]{0,1:T(1,128)}) fusion(s32[2,512]{1,0:T(2,128)S(1)} %copy-done.1, s32[]{:T(128)} %bitcast.7, s32[]{:T(128)} %bitcast), kind=kLoop, calls=%fused_computation.33 | loop fusion | flops 5120 | bytes 8200 | tf_op jit(solution)/shard_map/select_n | solution.py:88
  67.4 9.3 %all-gather.3.cloned.1.call-done = f32[256,2,1024]{2,1,0:T(2,128)} async-done(((f32[128,2,1024]{2,1,0:T(2,128)}), f32[256,2,1024]{2,1,0:T(2,128)}) %all-gather.3.cloned.1.call-update) | async-done | bytes 2097168 | tf_op jit(solution)/shard_map/all_gather | solution.py:67
  76.6 2.7 %reshape.96 = f32[512,1024]{1,0:T(8,128)S(1)} reshape(f32[256,2,1024]{2,1,0:T(2,128)} %all-gather.3.cloned.1.call-done) | data formatting | bytes 4194304 | tf_op jit(solution)/shard_map/reshape | solution.py:68
  79.4 0.0 copy-start.2
  79.4 2.6 %scatter_custom_fusion.1 = f32[512]{0:T(512)S(1)} fusion(s32[512]{0:T(512)} %bitcast.69, f32[512]{0:T(512)S(1)} %get-tuple-element.349, f32[]{:T(128)} %constant.224.clone.1), kind=kCustom, calls=%fused_computation.46 | custom fusion | bytes 2560 | tf_op jit(solution)/shard_map/scatter | solution.py:88
  82.0 0.0 copy-done.2
  82.0 0.0 copy-start
  82.0 2.4 %scatter_fusion.1 = f32[512]{0:T(512)S(1)} fusion(f32[512]{0:T(512)S(1)} %scatter_custom_fusion.1, s32[512]{0:T(512)S(1)} %bitcast.68, f32[512]{0:T(512)S(1)} %get-tuple-element.350), kind=kCustom, calls=%fused_computation.7 | custom fusion | bytes 8192 | tf_op jit(solution)/shard_map/scatter | solution.py:88
  84.4 0.1 reshape.97
  84.6 15.5 %pmax.7 = f32[2,128,2]{2,1,0:T(8,128)S(1)} all-reduce(f32[2,128,2]{2,1,0:T(8,128)S(1)} %reshape.97), channel_id=1, replica_groups=mesh['docs'=128,'tiles'=2] {'tiles'}, use_global_device_ids=true, to_apply=%region_15.16 | all-reduce | flops 512 | bytes 4096 | tf_op jit(solution)/shard_map/pmax | solution.py:89
  100.1 24.1 %all_to_all.18 = f32[128,1,2]{2,1,0:T(1,128)S(1)} all-to-all(f32[128,1,2]{2,1,0:T(1,128)S(1)} %bitcast.67), channel_id=1, replica_groups=mesh['docs'=128,'tiles'=2] {'docs'}, dimensions={0} | all-to-all | bytes 2048 | tf_op jit(solution)/shard_map/all_to_all | solution.py:93
  124.2 0.0 copy-done
  124.2 1.8 %gather_fusion.4 = f32[128]{0:T(128)} fusion(f32[128,2]{1,0:T(8,128)S(1)} %bitcast.64, s32[128]{0:T(128)S(1)} %copy-done), kind=kCustom, calls=%fused_computation.4 | custom fusion | bytes 2048 | tf_op jit(solution)/shard_map/gather | solution.py:94
  (7 shorter events, 0.1 us)
Async XLA Ops:
  6.5 70.1 %all-gather.3.cloned.1.call-start = ((), (), s32[]{:S(2)}) async-start(), calls=%async_computation.2 | async-start | bytes 3145728 | tf_op jit(solution)/shard_map/all_gather | solution.py:67
  18.7 44.9 %copy-start.3 = (s32[2]{0:T(128)S(1)}, s32[2]{0:T(128)}, u32[]{:S(2)}) copy-start(s32[2]{0:T(128)} %param.15) | copy-start | bytes 28
  18.8 46.8 %copy-start.1 = (s32[2,512]{1,0:T(2,128)S(1)}, s32[2,512]{1,0:T(2,128)}, u32[]{:S(2)}) copy-start(s32[2,512]{1,0:T(2,128)} %param.14) | copy-start | bytes 12292
  79.4 2.6 %copy-start.2 = (s32[512,1]{0,1:T(1,128)S(1)}, s32[512,1]{0,1:T(1,128)}, u32[]{:S(2)}) copy-start(s32[512,1]{0,1:T(1,128)} %get-tuple-element.441) | copy-start | bytes 6148
  82.0 42.2 %copy-start = (s32[128]{0:T(128)S(1)}, s32[128]{0:T(128)}, u32[]{:S(2)}) copy-start(s32[128]{0:T(128)} %get-tuple-element.443) | copy-start | bytes 1540
Sparse Core Ops, SparseCore 0:
  63.8 12.8 all-gather.2
where the time goes:
time: 133 us
  blocking collectives  84.4 us (63%)
  local copies, waits for them, and re-layouts  18 us (14%)
  between operations  14.9 us (11%)
  waiting for transfers between devices  9.28 us (7%)
  other arithmetic  6.22 us (5%)
    all_to_all x1, blocking collectives, local(): lax.all_to_all(outgoing, 'docs', split_axis=0, concat_axis=0, tiled=True)  44.9 us
    all_to_all x1, blocking collectives, local(): lax.all_to_all(own_half, 'docs', split_axis=0, concat_axis=0, tiled=True)  24.1 us
    pmax x1, blocking collectives, local(): merged = lax.pmax(place_max, 'tiles')  15.5 us
    all_gather x1, waiting for transfers between devices, local(): buffer = lax.all_gather(received[None], 'tiles', axis=0, tiled=True)  9.26 us
    scatter x1, local copies, waits for them, and re-layouts, local(): outgoing = jnp.zeros((n_docs, send_cap, feat_width), jnp.float32).at[home...  7.49 us
    scatter x2, local copies, waits for them, and re-layouts, local(): place_max = place_max.at[target].set(maxima, mode='drop')  5 us
    reshape x1, local copies, waits for them, and re-layouts, local(): flat_rows = buffer.reshape(-1, feat_width)  2.69 us
  transfers between devices with their start and end apart: 1, of which 1 were waited for; matrix products, arithmetic and copies ran while one was open for 2% of the time, Pallas kernels for 0%

commit v1 on v0

v1 whole, which is shorter than its diff:
```python
import functools

import jax
import jax.numpy as jnp
from jax import lax
from jax.experimental import pallas as pl
from jax.experimental.pallas import tpu as pltpu
from jax.sharding import PartitionSpec as P

EPS = 1e-06
LANES = 128
PARAMS = pltpu.CompilerParams(vmem_limit_bytes=32 * 1024 * 1024)


def parts_of(rows):
    high = rows.astype(jnp.bfloat16)
    rest = rows - high.astype(jnp.float32)
    return high, rest


def prep_kernel(cl_local, send_cap, cluster_ref, rows_ref, out_ref, slot_ref):
    docs, width = rows_ref.shape
    slots = out_ref.shape[0] * LANES // width
    chunks = width // LANES
    home = lax.shift_right_logical(cluster_ref[...], cl_local.bit_length() - 1)
    across = jnp.broadcast_to(home, (docs, docs))
    down = across.T
    sub = lax.broadcasted_iota(jnp.int32, (docs, docs), 0)
    lane = lax.broadcasted_iota(jnp.int32, (docs, docs), 1)
    before = jnp.where((across == down) & (sub < lane), 1, 0)
    slot = home * send_cap + jnp.sum(before, axis=0, keepdims=True)
    slot_ref[...] = slot
    place = lax.broadcasted_iota(jnp.int32, (slots, docs), 0)
    chosen = jnp.where(place == slot, 1.0, 0.0).astype(jnp.bfloat16)
    rows = rows_ref[...]
    unit = rows * lax.rsqrt(jnp.sum(rows * rows, axis=1, keepdims=True) + EPS)
    high, rest = parts_of(unit)
    middle, rest = parts_of(rest)
    low = rest.astype(jnp.bfloat16)

    def put(part):
        return jnp.dot(chosen, part, preferred_element_type=jnp.float32)

    placed = put(high) + put(middle) + put(low)
    for chunk in range(chunks):
        out_ref[pl.ds(chunk, slots, stride=chunks), :] = placed[
            :, chunk * LANES : (chunk + 1) * LANES
        ]


def split_rows(rows_ref, high_ref, low_ref, send_cap):
    count, width = high_ref.shape
    chunks = width // LANES
    each = count // send_cap
    for rank in range(send_cap):
        for chunk in range(chunks):
            part = rows_ref[pl.ds(rank * chunks + chunk, each, stride=send_cap * chunks), :]
            high, rest = parts_of(part)
            cols = slice(chunk * LANES, (chunk + 1) * LANES)
            high_ref[rank * each : (rank + 1) * each, cols] = high
            low_ref[rank * each : (rank + 1) * each, cols] = rest.astype(jnp.bfloat16)


def codes_of(lists, counts, half, rows, send_cap):
    cap = lists.shape[1]
    each = rows // send_cap
    row = lax.broadcasted_iota(jnp.int32, (rows, 1), 0)
    rank = row // each
    place = half * rows + (row - rank * each) * send_cap + rank
    position = lax.broadcasted_iota(jnp.int32, (1, cap), 1)
    code = jnp.full((rows, cap), -1, jnp.int32)
    for cluster in range(lists.shape[0]):
        listed = jnp.where(position < counts[cluster], lists[cluster : cluster + 1, :], -1)
        code = jnp.where(listed == place, position + cluster * cap, code)
    return jnp.max(code, axis=1, keepdims=True)


def across_lanes(column):
    wide = jnp.broadcast_to(column, (column.shape[0], LANES))
    return wide.T[:1, :]


def nt(left, right):
    return lax.dot_general(
        left, right, (((1,), (1,)), ((), ())), preferred_element_type=jnp.float32
    )


def best_of(q_high, q_low, k_high, k_low, q_code, k_code, cap):
    scores = nt(q_high, k_high) + (nt(q_high, k_low) + nt(q_low, k_high))
    first = q_code // cap * cap
    allowed = (k_code < q_code) & (k_code >= first)
    return jnp.max(jnp.where(allowed, scores, -1.0), axis=1, keepdims=True)


def gram_kernel(send_cap, lists_ref, counts_ref, core_ref, own_ref, other_ref, out_ref,
                own_high, own_low, other_high, other_low):
    rows = own_high.shape[0]
    each = rows // send_cap
    cap = lists_ref.shape[1]
    lists = lists_ref[...]
    counts = [counts_ref[index] for index in range(lists.shape[0])]
    core = core_ref[0]
    own_code = codes_of(lists, counts, core, rows, send_cap)
    other_code = codes_of(lists, counts, 1 - core, rows, send_cap)
    split_rows(own_ref, own_high, own_low, send_cap)
    split_rows(other_ref, other_high, other_low, send_cap)
    q_high, q_low = own_high[...], own_low[...]
    best = best_of(q_high, q_low, q_high, q_low, own_code, across_lanes(own_code), cap)
    best = jnp.maximum(
        best,
        best_of(q_high, q_low, other_high[...], other_low[...], own_code,
                across_lanes(other_code), cap),
    )
    lane = lax.broadcasted_iota(jnp.int32, (each, LANES), 1)
    out = jnp.broadcast_to(best[:each], (each, LANES))
    for rank in range(1, send_cap):
        out = jnp.where(lane == rank, best[rank * each : (rank + 1) * each], out)
    out_ref[...] = out


def pick_kernel(send_cap, slot_ref, back_ref, out_ref):
    homes = back_ref.shape[0]
    docs = slot_ref.shape[1]
    slot = slot_ref[...]
    home = lax.broadcasted_iota(jnp.int32, (homes, docs), 0)
    back = back_ref[...]
    picked = jnp.zeros((homes, docs), jnp.float32)
    for rank in range(send_cap):
        value = jnp.broadcast_to(back[:, rank : rank + 1], (homes, docs))
        picked = jnp.where(slot == home * send_cap + rank, value, picked)
    out_ref[...] = jnp.sum(picked, axis=0, keepdims=True)


def local(embeddings, cluster_of, row_lists, row_counts):
    n_docs = lax.axis_size("docs")
    n_tiles = lax.axis_size("tiles")
    doc_count, width = embeddings.shape
    send_cap = n_tiles * doc_count // n_docs
    cl_local = row_lists.shape[0]
    core = lax.axis_index("tiles").astype(jnp.int32).reshape(1)
    slots = n_docs * send_cap
    flat = (slots * width // LANES, LANES)
    vmem = pl.BlockSpec(memory_space=pltpu.VMEM)
    smem = pl.BlockSpec(memory_space=pltpu.SMEM)

    outgoing, slot = pl.pallas_call(
        functools.partial(prep_kernel, cl_local, send_cap),
        out_shape=(
            jax.ShapeDtypeStruct(flat, jnp.float32),
            jax.ShapeDtypeStruct((1, doc_count), jnp.int32),
        ),
        in_specs=[vmem, vmem],
        out_specs=(vmem, vmem),
        compiler_params=PARAMS,
        name="prep",
    )(cluster_of.reshape(1, doc_count), embeddings)

    def exchange(blocks):
        return lax.all_to_all(blocks, "docs", split_axis=0, concat_axis=0, tiled=True)

    own = exchange(outgoing.reshape(n_docs, -1, LANES)).reshape(flat)
    other = lax.ppermute(own, "tiles", [(0, 1), (1, 0)])

    half = pltpu.VMEM((slots, width), jnp.bfloat16)
    best = pl.pallas_call(
        functools.partial(gram_kernel, send_cap),
        out_shape=jax.ShapeDtypeStruct((n_docs, LANES), jnp.float32),
        in_specs=[vmem, smem, smem, vmem, vmem],
        out_specs=vmem,
        scratch_shapes=[half, half, half, half],
        compiler_params=PARAMS,
        name="gram",
    )(row_lists, row_counts, core, own, other)

    back = exchange(best.reshape(n_docs, 1, LANES)).reshape(n_docs, LANES)
    picked = pl.pallas_call(
        functools.partial(pick_kernel, send_cap),
        out_shape=jax.ShapeDtypeStruct((1, doc_count), jnp.float32),
        in_specs=[vmem, vmem],
        out_specs=vmem,
        compiler_params=PARAMS,
        name="pick",
    )(slot, back)
    return picked.reshape(doc_count)


def solution(mesh):
    placed = (P(("docs", "tiles"), None), P(("docs", "tiles")), P("docs", None), P("docs"))
    return jax.shard_map(
        local, mesh=mesh, in_specs=placed, out_specs=P(("docs", "tiles")), check_vma=False
    )
```

time: 133 us -> 72.9 us (0.55)
  blocking collectives: 84.4 us -> 61.1 us
  local copies, waits for them, and re-layouts: 18 us -> 1.7 us
  between operations: 14.9 us -> 0.02 us
  waiting for transfers between devices: 9.28 us -> 2.28 us
  other arithmetic: 6.22 us -> 0 us
  Pallas kernels: 0 us -> 4.05 us
  starting transfers between devices: 0.01 us -> 3.53 us
    pmax x1 -> x0, blocking collectives: 15.5 us -> none  [local(): merged = lax.pmax(place_max, 'tiles')]
    scatter x3 -> x0, local copies, waits for them, and re-layouts: 12.5 us -> none  [the longest x1 7.49 us: local(): outgoing = jnp.zeros((n_docs, send_cap, feat_width), jnp.float32).at[home...]
    all_gather x1 -> x0, waiting for transfers between devices: 9.26 us -> none  [local(): buffer = lax.all_gather(received[None], 'tiles', axis=0, tiled=True)]
    all_to_all x2, blocking collectives: 68.9 us -> 61.1 us  [exchange(): lax.all_to_all(blocks, 'docs', split_axis=0, concat_axis=0, tiled=True)]
    pallas_call x0 -> x3, Pallas kernels: none -> 4.05 us  [the longest x1 2.66 us: local(): pl.pallas_call(functools.partial(gram_kernel, send_cap), out_shape=jax.Sh...]
    ppermute x0 -> x1, starting transfers between devices: none -> 3.53 us  [local(): other = lax.ppermute(own, 'tiles', [(0, 1), (1, 0)])]
    reshape x2 -> x0, local copies, waits for them, and re-layouts: 2.83 us -> none  [the longest x1 2.69 us: local(): flat_rows = buffer.reshape(-1, feat_width)]
    select_n x2 -> x0, other arithmetic: 2.45 us -> none  [the longest x1 1.79 us: local(): place_max = place_max.at[target].set(maxima, mode='drop')]
  transfers between devices with their start and end apart: 1 -> 1, of which waited for: 1 -> 1; matrix products, arithmetic and copies ran while one was open for 2% -> 0% of each run, Pallas kernels for 0% -> 0%
where the time goes in v1:
time: 72.9 us; the launch traced here: 72.7 us
  blocking collectives  61.1 us (84%)
  Pallas kernels  4.05 us (6%)
  starting transfers between devices  3.53 us (5%)
  waiting for transfers between devices  2.28 us (3%)
  local copies, waits for them, and re-layouts  1.7 us (2%)
    all_to_all x2, blocking collectives, exchange(): lax.all_to_all(blocks, 'docs', split_axis=0, concat_axis=0, tiled=True)  61.1 us
    ppermute x1, starting transfers between devices, local(): other = lax.ppermute(own, 'tiles', [(0, 1), (1, 0)])  3.53 us
    pallas_call x1, Pallas kernels, local(): pl.pallas_call(functools.partial(gram_kernel, send_cap), out_shape=jax.Sh...  2.66 us
    ppermute x1, waiting for transfers between devices, local(): other = lax.ppermute(own, 'tiles', [(0, 1), (1, 0)])  2.28 us
    unnamed x8, local copies, waits for them, and re-layouts  1.7 us
  transfers between devices with their start and end apart: 1, of which 1 were waited for; matrix products, arithmetic and copies ran while one was open for 0% of the time, Pallas kernels for 0%

profile of v1, /device:TPU:1, one launch (start us, length us, event | category | flops | bytes accessed | tf_op | source)
XLA Modules:
  0.0 72.7 jit_solution(3626115077474592080)
XLA Ops:
  0.0 0.0 copy-start.2
  0.0 0.7 copy-done.2
  0.7 0.0 copy-start
  0.7 1.0 %copy-done = f32[128,1024]{1,0:T(8,128)S(1)} copy-done((f32[128,1024]{1,0:T(8,128)S(1)}, f32[128,1024]{1,0:T(8,128)}, u32[]{:S(2)}) %copy-start) | copy-done | bytes 524312
  1.7 0.8 %prep.1 = (f32[2048,128]{1,0:T(8,128)S(1)}, s32[1,128]{1,0:T(1,128)S(1)}) custom-call(s32[1,128]{1,0:T(1,128)S(1)} %bitcast.14, f32[128,1024]{1,0:T(8,128)S(1)} %copy-done), custom_call_target="tpu_custom_call" | custom-call | tf_op jit(solution)/shard_map/prep/pallas_call | solution.py:147
  2.5 44.7 %all_to_all.10 = f32[128,16,128]{2,1,0:T(8,128)S(1)} all-to-all(f32[128,16,128]{2,1,0:T(8,128)S(1)} %bitcast.11), channel_id=1, replica_groups=mesh['docs'=128,'tiles'=2] {'docs'}, dimensions={0} | all-to-all | bytes 2097152 | tf_op jit(solution)/shard_map/all_to_all | solution.py:160
  47.2 0.0 copy-start.1
  47.2 3.5 %collective-permute-start = (f32[2048,128]{1,0:T(8,128)S(1)}, f32[2048,128]{1,0:T(8,128)S(1)}, u32[]{:S(2)}, u32[]{:S(2)}) collective-permute-start(f32[2048,128]{1,0:T(8,128)S(1)} %bitcast.9), channel_id=1, source_target_pairs={{0,1},{1,0},{2,3},{3,2},{4,5},{5,4},{6,7},{7,6},{8,9},{9,8},{10,11... | collective-permute-start | bytes 3145736 | tf_op jit(solution)/shard_map/ppermute | solution.py:163
  50.8 0.0 copy-start.3
  50.8 2.3 %collective-permute-done.other_ref = f32[2048,128]{1,0:T(8,128)S(1)} collective-permute-done((f32[2048,128]{1,0:T(8,128)S(1)}, f32[2048,128]{1,0:T(8,128)S(1)}, u32[]{:S(2)}, u32[]{:S(2)}) %collective-permute-start) | collective-permute-done | bytes 1048608 | tf_op jit(solution)/shard_map/ppermute | solution.py:163
  53.0 0.0 copy-done.1
  53.0 0.0 copy-done.3
  53.0 2.7 %gram.1 = f32[128,128]{1,0:T(8,128)S(1)} custom-call(s32[2,512]{1,0:T(2,128)S(1)} %copy-done.1, s32[2]{0:T(128)S(1)} %copy-done.3, s32[1]{0:T(128)} %bitcast.1.core_ref, f32[2048,128]{1,0:T(8,128)S(1)} %bitcast.10, f32[2048,128]{1,0:T(8,128)S(1)} %collective-permute-done.other_ref), custom_call_target="tpu_custom_call" | custom-call | tf_op jit(solution)/shard_map/gram/pallas_call | solution.py:166
  55.7 16.4 %all_to_all.11 = f32[128,1,128]{2,1,0:T(1,128)S(1)} all-to-all(f32[128,1,128]{2,1,0:T(1,128)S(1)} %bitcast.12), channel_id=1, replica_groups=mesh['docs'=128,'tiles'=2] {'docs'}, dimensions={0} | all-to-all | bytes 131072 | tf_op jit(solution)/shard_map/all_to_all | solution.py:160
  72.1 0.6 pick.1
Async XLA Ops:
  0.0 0.7 copy-start.2
  0.7 1.0 %copy-start = (f32[128,1024]{1,0:T(8,128)S(1)}, f32[128,1024]{1,0:T(8,128)}, u32[]{:S(2)}) copy-start(f32[128,1024]{1,0:T(8,128)} %rows_ref.1) | copy-start | bytes 1572868
  47.2 5.8 %copy-start.1 = (s32[2,512]{1,0:T(2,128)S(1)}, s32[2,512]{1,0:T(2,128)}, u32[]{:S(2)}) copy-start(s32[2,512]{1,0:T(2,128)} %lists_ref.1) | copy-start | bytes 12292
  47.2 5.8 %collective-permute-start = (f32[2048,128]{1,0:T(8,128)S(1)}, f32[2048,128]{1,0:T(8,128)S(1)}, u32[]{:S(2)}, u32[]{:S(2)}) collective-permute-start(f32[2048,128]{1,0:T(8,128)S(1)} %bitcast.9), channel_id=1, source_target_pairs={{0,1},{1,0},{2,3},{3,2},{4,5},{5,4},{6,7},{7,6},{8,9},{9,8},{10,11... | collective-permute-start | bytes 3145736 | tf_op jit(solution)/shard_map/ppermute | solution.py:163
  50.8 2.3 %copy-start.3 = (s32[2]{0:T(128)S(1)}, s32[2]{0:T(128)}, u32[]{:S(2)}) copy-start(s32[2]{0:T(128)} %counts_ref.1) | copy-start | bytes 28

commit v2 on v1

--- a/solution.py
+++ b/solution.py
@@ -9,7 +9,13 @@
 
 EPS = 1e-06
 LANES = 128
+PIECES = 4
+FIRST = 74
 PARAMS = pltpu.CompilerParams(vmem_limit_bytes=32 * 1024 * 1024)
+
+
+def regroup(index):
+    return index ^ FIRST
 
 
 def parts_of(rows):
@@ -18,23 +24,39 @@
     return high, rest
 
 
-def prep_kernel(cl_local, send_cap, cluster_ref, rows_ref, out_ref, slot_ref):
+def prep_kernel(cl_local, send_cap, cluster_hbm, rows_hbm, out_ref, slot_ref,
+                cluster_ref, rows_ref, cluster_sem, rows_sems):
     docs, width = rows_ref.shape
     slots = out_ref.shape[0] * LANES // width
     chunks = width // LANES
+    pieces = rows_sems.shape[0]
+    piece = docs // pieces
+    cluster_copy = pltpu.make_async_copy(cluster_hbm, cluster_ref, cluster_sem)
+    cluster_copy.start()
+    copies = []
+    for index in range(pieces):
+        span = pl.ds(index * piece, piece)
+        copies.append(
+            pltpu.make_async_copy(rows_hbm.at[span], rows_ref.at[span], rows_sems.at[index])
+        )
+        copies[-1].start()
+    cluster_copy.wait()
     home = lax.shift_right_logical(cluster_ref[...], cl_local.bit_length() - 1)
     across = jnp.broadcast_to(home, (docs, docs))
     down = across.T
     sub = lax.broadcasted_iota(jnp.int32, (docs, docs), 0)
     lane = lax.broadcasted_iota(jnp.int32, (docs, docs), 1)
     before = jnp.where((across == down) & (sub < lane), 1, 0)
-    slot = home * send_cap + jnp.sum(before, axis=0, keepdims=True)
+    slot = regroup(home) * send_cap + jnp.sum(before, axis=0, keepdims=True)
     slot_ref[...] = slot
     place = lax.broadcasted_iota(jnp.int32, (slots, docs), 0)
     chosen = jnp.where(place == slot, 1.0, 0.0).astype(jnp.bfloat16)
-    rows = rows_ref[...]
-    unit = rows * lax.rsqrt(jnp.sum(rows * rows, axis=1, keepdims=True) + EPS)
-    high, rest = parts_of(unit)
+    units = []
+    for index in range(pieces):
+        copies[index].wait()
+        rows = rows_ref[index * piece : (index + 1) * piece, :]
+        units.append(rows * lax.rsqrt(jnp.sum(rows * rows, axis=1, keepdims=True) + EPS))
+    high, rest = parts_of(jnp.concatenate(units, axis=0))
     middle, rest = parts_of(rest)
     low = rest.astype(jnp.bfloat16)
 
@@ -66,7 +88,7 @@
     each = rows // send_cap
     row = lax.broadcasted_iota(jnp.int32, (rows, 1), 0)
     rank = row // each
-    place = half * rows + (row - rank * each) * send_cap + rank
+    place = half * rows + regroup(row - rank * each) * send_cap + rank
     position = lax.broadcasted_iota(jnp.int32, (1, cap), 1)
     code = jnp.full((rows, cap), -1, jnp.int32)
     for cluster in range(lists.shape[0]):
@@ -93,24 +115,30 @@
     return jnp.max(jnp.where(allowed, scores, -1.0), axis=1, keepdims=True)
 
 
-def gram_kernel(send_cap, lists_ref, counts_ref, core_ref, own_ref, other_ref, out_ref,
-                own_high, own_low, other_high, other_low):
-    rows = own_high.shape[0]
-    each = rows // send_cap
+def near_kernel(send_cap, lists_ref, counts_ref, core_ref, own_ref,
+                high_ref, low_ref, own_code_ref, other_code_ref, best_ref):
+    rows = high_ref.shape[0]
     cap = lists_ref.shape[1]
     lists = lists_ref[...]
     counts = [counts_ref[index] for index in range(lists.shape[0])]
     core = core_ref[0]
     own_code = codes_of(lists, counts, core, rows, send_cap)
-    other_code = codes_of(lists, counts, 1 - core, rows, send_cap)
-    split_rows(own_ref, own_high, own_low, send_cap)
+    own_code_ref[...] = own_code
+    other_code_ref[...] = across_lanes(codes_of(lists, counts, 1 - core, rows, send_cap))
+    split_rows(own_ref, high_ref, low_ref, send_cap)
+    high, low = high_ref[...], low_ref[...]
+    best_ref[...] = best_of(high, low, high, low, own_code, across_lanes(own_code), cap)
+
+
+def far_kernel(send_cap, cap, high_ref, low_ref, own_code_ref, other_code_ref, best_ref,
+               other_ref, out_ref, other_high, other_low):
+    rows = high_ref.shape[0]
+    each = rows // send_cap
     split_rows(other_ref, other_high, other_low, send_cap)
-    q_high, q_low = own_high[...], own_low[...]
-    best = best_of(q_high, q_low, q_high, q_low, own_code, across_lanes(own_code), cap)
     best = jnp.maximum(
-        best,
-        best_of(q_high, q_low, other_high[...], other_low[...], own_code,
-                across_lanes(other_code), cap),
+        best_ref[...],
+        best_of(high_ref[...], low_ref[...], other_high[...], other_low[...],
+                own_code_ref[...], other_code_ref[...], cap),
     )
     lane = lax.broadcasted_iota(jnp.int32, (each, LANES), 1)
     out = jnp.broadcast_to(best[:each], (each, LANES))
@@ -144,34 +172,62 @@
     vmem = pl.BlockSpec(memory_space=pltpu.VMEM)
     smem = pl.BlockSpec(memory_space=pltpu.SMEM)
 
+    hbm = pl.BlockSpec(memory_space=pltpu.HBM)
+
+    def in_hbm(array):
+        return pltpu.with_memory_space_constraint(array, pltpu.HBM)
+
     outgoing, slot = pl.pallas_call(
         functools.partial(prep_kernel, cl_local, send_cap),
         out_shape=(
             jax.ShapeDtypeStruct(flat, jnp.float32),
             jax.ShapeDtypeStruct((1, doc_count), jnp.int32),
         ),
-        in_specs=[vmem, vmem],
+        in_specs=[hbm, hbm],
         out_specs=(vmem, vmem),
+        scratch_shapes=[
+            pltpu.VMEM((1, doc_count), jnp.int32),
+            pltpu.VMEM((doc_count, width), jnp.float32),
+            pltpu.SemaphoreType.DMA,
+            pltpu.SemaphoreType.DMA((PIECES,)),
+        ],
         compiler_params=PARAMS,
         name="prep",
-    )(cluster_of.reshape(1, doc_count), embeddings)
+    )(in_hbm(cluster_of.reshape(1, doc_count)), in_hbm(embeddings))
 
     def exchange(blocks):
-        return lax.all_to_all(blocks, "docs", split_axis=0, concat_axis=0, tiled=True)
+        return lax.all_to_all(
+            blocks, "docs", split_axis=0, concat_axis=0, tiled=True,
+            axis_index_groups=[[regroup(index) for index in range(n_docs)]],
+        )
 
     own = exchange(outgoing.reshape(n_docs, -1, LANES)).reshape(flat)
     other = lax.ppermute(own, "tiles", [(0, 1), (1, 0)])
 
-    half = pltpu.VMEM((slots, width), jnp.bfloat16)
+    half = jax.ShapeDtypeStruct((slots, width), jnp.bfloat16)
+    near = pl.pallas_call(
+        functools.partial(near_kernel, send_cap),
+        out_shape=(
+            half,
+            half,
+            jax.ShapeDtypeStruct((slots, 1), jnp.int32),
+            jax.ShapeDtypeStruct((1, slots), jnp.int32),
+            jax.ShapeDtypeStruct((slots, 1), jnp.float32),
+        ),
+        in_specs=[vmem, smem, smem, vmem],
+        out_specs=(vmem,) * 5,
+        compiler_params=PARAMS,
+        name="near",
+    )(row_lists, row_counts, core, own)
     best = pl.pallas_call(
-        functools.partial(gram_kernel, send_cap),
+        functools.partial(far_kernel, send_cap, row_lists.shape[1]),
         out_shape=jax.ShapeDtypeStruct((n_docs, LANES), jnp.float32),
-        in_specs=[vmem, smem, smem, vmem, vmem],
+        in_specs=[vmem] * 6,
         out_specs=vmem,
-        scratch_shapes=[half, half, half, half],
-        compiler_params=PARAMS,
-        name="gram",
-    )(row_lists, row_counts, core, own, other)
+        scratch_shapes=[pltpu.VMEM((slots, width), jnp.bfloat16)] * 2,
+        compiler_params=PARAMS,
+        name="far",
+    )(*near, other)
 
     back = exchange(best.reshape(n_docs, 1, LANES)).reshape(n_docs, LANES)
     picked = pl.pallas_call(

time: 72.9 us -> 64.5 us (0.88)
  blocking collectives: 61.1 us -> 56.8 us
  starting transfers between devices: 3.53 us -> 1.25 us
  waiting for transfers between devices: 2.28 us -> 0.01 us
  Pallas kernels: 4.05 us -> 5.61 us
  local copies, waits for them, and re-layouts: 1.7 us -> 0.66 us
    all_to_all x2, blocking collectives: 61.1 us -> 56.8 us  [exchange(): lax.all_to_all(blocks, 'docs', split_axis=0, concat_axis=0, tiled=True, a...]
    ppermute x1, waiting for transfers between devices: 2.28 us -> 0.01 us  [local(): other = lax.ppermute(own, 'tiles', [(0, 1), (1, 0)])]
    ppermute x1, starting transfers between devices: 3.53 us -> 1.25 us  [local(): other = lax.ppermute(own, 'tiles', [(0, 1), (1, 0)])]
    pallas_call x1, Pallas kernels: 0.78 us -> 1.98 us  [local(): pl.pallas_call(functools.partial(prep_kernel, cl_local, send_cap), out_sh...]
    unnamed x8 -> x4, local copies, waits for them, and re-layouts: 1.7 us -> 0.66 us
    pallas_call x1 -> x2, Pallas kernels: 2.66 us -> 3.01 us  [the longest x1 1.87 us: local(): pl.pallas_call(functools.partial(near_kernel, send_cap), out_shape=(half,...]
  transfers between devices with their start and end apart: 1 -> 1, of which waited for: 1 -> 0; matrix products, arithmetic and copies ran while one was open for 0% -> 0% of each run, Pallas kernels for 0% -> 3%
where the time goes in v2:
time: 64.5 us; the launch traced here: 64.3 us
  blocking collectives  56.8 us (88%)
  Pallas kernels  5.61 us (9%)
  starting transfers between devices  1.25 us (2%)
  local copies, waits for them, and re-layouts  0.66 us (1%)
    all_to_all x2, blocking collectives, exchange(): lax.all_to_all(blocks, 'docs', split_axis=0, concat_axis=0, tiled=True, a...  56.8 us
    pallas_call x1, Pallas kernels, local(): pl.pallas_call(functools.partial(prep_kernel, cl_local, send_cap), out_sh...  1.98 us
    pallas_call x1, Pallas kernels, local(): pl.pallas_call(functools.partial(near_kernel, send_cap), out_shape=(half,...  1.87 us
  transfers between devices with their start and end apart: 1, of which 0 were waited for; matrix products, arithmetic and copies ran while one was open for 0% of the time, Pallas kernels for 3%

profile of v2, /device:TPU:1, one launch (start us, length us, event | category | flops | bytes accessed | tf_op | source)
XLA Modules:
  0.0 64.3 jit_solution(1765019885151694499)
XLA Ops:
  0.0 2.0 %prep.1 = (f32[2048,128]{1,0:T(8,128)S(1)}, s32[1,128]{1,0:T(1,128)S(1)}) custom-call(s32[1,128]{1,0:T(1,128)} %bitcast.14, f32[128,1024]{1,0:T(8,128)} %rows_hbm.1), custom_call_target="tpu_custom_call" | custom-call | tf_op jit(solution)/shard_map/prep/pallas_call | solution.py:180
  2.0 41.0 %all_to_all.10 = f32[128,16,128]{2,1,0:T(8,128)S(1)} all-to-all(f32[128,16,128]{2,1,0:T(8,128)S(1)} %bitcast.11), channel_id=1, replica_groups={{148,150,144,146,156,158,152,154,132,134,128,130,140,142,136,138,180,18..., dimensions={0} | all-to-all | bytes 2097152 | tf_op jit(solution)/shard_map/all_to_all | solution.py:199
  43.0 0.0 copy-start
  43.0 1.3 %collective-permute-start = (f32[2048,128]{1,0:T(8,128)S(1)}, f32[2048,128]{1,0:T(8,128)S(1)}, u32[]{:S(2)}, u32[]{:S(2)}) collective-permute-start(f32[2048,128]{1,0:T(8,128)S(1)} %bitcast.9), channel_id=1, source_target_pairs={{0,1},{1,0},{2,3},{3,2},{4,5},{5,4},{6,7},{7,6},{8,9},{9,8},{10,11... | collective-permute-start | bytes 3145736 | tf_op jit(solution)/shard_map/ppermute | solution.py:205
  44.2 0.0 copy-start.1
  44.2 0.0 copy-done
  44.3 0.7 %copy-done.1 = s32[2]{0:T(128)S(1)} copy-done((s32[2]{0:T(128)S(1)}, s32[2]{0:T(128)}, u32[]{:S(2)}) %copy-start.1) | copy-done | bytes 32
  44.9 1.9 %near.1 = (bf16[256,1024]{1,0:T(8,128)(2,1)S(1)}, bf16[256,1024]{1,0:T(8,128)(2,1)S(1)}, s32[256,1]{1,0:T(8,128)S(1)}, s32[1,256]{1,0:T(1,128)S(1)}, f32[256,1]{1,0:T(8,128)S(1)}) custom-call(s32[2,512]{1,0:T(2,128)S(1)} %copy-done, s32[2]{0:T(128)S(1)} %copy-done.1, s32[1]{0:T(128)} %bitcast.1.core_ref, f32[2048,128]{1,0:T(8,128)S(1)} %bitcast.10), custom_call_target="tpu_custom_call" | custom-call | tf_op jit(solution)/shard_map/near/pallas_call | solution.py:208
  46.8 0.0 collective-permute-done.other_ref
  46.8 1.1 %far.1 = f32[128,128]{1,0:T(8,128)S(1)} custom-call(bf16[256,1024]{1,0:T(8,128)(2,1)S(1)} %get-tuple-element.14.high_ref, bf16[256,1024]{1,0:T(8,128)(2,1)S(1)} %get-tuple-element.15.low_ref, s32[256,1]{1,0:T(8,128)S(1)} %get-tuple-element.16.own_code_ref, s32[1,256]{1,0:T(1,128)S(1)} %get-tuple-element.17.other_code_ref, ...), custom_call_target="tpu_custom_call" | custom-call | tf_op jit(solution)/shard_map/far/pallas_call | solution.py:222
  47.9 15.8 %all_to_all.11 = f32[128,1,128]{2,1,0:T(1,128)S(1)} all-to-all(f32[128,1,128]{2,1,0:T(1,128)S(1)} %bitcast.12), channel_id=1, replica_groups={{148,150,144,146,156,158,152,154,132,134,128,130,140,142,136,138,180,18..., dimensions={0} | all-to-all | bytes 131072 | tf_op jit(solution)/shard_map/all_to_all | solution.py:199
  63.7 0.6 pick.1
Async XLA Ops:
  43.0 1.3 %copy-start = (s32[2,512]{1,0:T(2,128)S(1)}, s32[2,512]{1,0:T(2,128)}, u32[]{:S(2)}) copy-start(s32[2,512]{1,0:T(2,128)} %lists_ref.1) | copy-start | bytes 12292
  43.0 3.8 %collective-permute-start = (f32[2048,128]{1,0:T(8,128)S(1)}, f32[2048,128]{1,0:T(8,128)S(1)}, u32[]{:S(2)}, u32[]{:S(2)}) collective-permute-start(f32[2048,128]{1,0:T(8,128)S(1)} %bitcast.9), channel_id=1, source_target_pairs={{0,1},{1,0},{2,3},{3,2},{4,5},{5,4},{6,7},{7,6},{8,9},{9,8},{10,11... | collective-permute-start | bytes 3145736 | tf_op jit(solution)/shard_map/ppermute | solution.py:205
  44.2 0.7 %copy-start.1 = (s32[2]{0:T(128)S(1)}, s32[2]{0:T(128)}, u32[]{:S(2)}) copy-start(s32[2]{0:T(128)} %counts_ref.1) | copy-start | bytes 28

commit v3 on v2

v3 whole, which is shorter than its diff:
```python
import functools

import jax
import jax.numpy as jnp
from jax import lax
from jax.experimental import pallas as pl
from jax.experimental.pallas import tpu as pltpu
from jax.sharding import PartitionSpec as P

EPS = 1e-06
LANES = 128
FIRST = 74
PARAMS = pltpu.CompilerParams(vmem_limit_bytes=32 * 1024 * 1024)


def regroup(index):
    return index ^ FIRST


def parts_of(rows):
    high = rows.astype(jnp.bfloat16)
    rest = rows - high.astype(jnp.float32)
    return high, rest


def codes_of(lists, counts, half, rows, send_cap):
    cap = lists.shape[1]
    each = rows // send_cap
    row = lax.broadcasted_iota(jnp.int32, (rows, 1), 0)
    rank = row // each
    place = half * rows + regroup(row - rank * each) * send_cap + rank
    position = lax.broadcasted_iota(jnp.int32, (1, cap), 1)
    code = jnp.full((rows, cap), -1, jnp.int32)
    for cluster in range(lists.shape[0]):
        listed = jnp.where(position < counts[:, cluster : cluster + 1],
                           lists[cluster : cluster + 1, :], -1)
        code = jnp.where(listed == place, position + cluster * cap, code)
    return jnp.max(code, axis=1, keepdims=True)


def prep_kernel(cl_local, send_cap, cluster_hbm, lists_hbm, counts_hbm, rows_hbm,
                out_ref, slot_ref, lists_ref, counts_ref, cluster_ref, rows_ref, sems):
    docs, width = rows_ref.shape
    slots = out_ref.shape[0] * LANES // width
    chunks = width // LANES
    copies = [
        pltpu.make_async_copy(source, target, sems.at[index])
        for index, (source, target) in enumerate(
            (
                (cluster_hbm, cluster_ref),
                (lists_hbm, lists_ref),
                (counts_hbm, counts_ref),
                (rows_hbm, rows_ref),
            )
        )
    ]
    for copy in copies:
        copy.start()
    copies[0].wait()
    home = lax.shift_right_logical(cluster_ref[...], cl_local.bit_length() - 1)
    across = jnp.broadcast_to(home, (docs, docs))
    down = across.T
    sub = lax.broadcasted_iota(jnp.int32, (docs, docs), 0)
    lane = lax.broadcasted_iota(jnp.int32, (docs, docs), 1)
    before = jnp.where((across == down) & (sub < lane), 1, 0)
    slot = regroup(home) * send_cap + jnp.sum(before, axis=0, keepdims=True)
    slot_ref[...] = slot
    place = lax.broadcasted_iota(jnp.int32, (slots, docs), 0)
    chosen = jnp.where(place == slot, 1.0, 0.0).astype(jnp.bfloat16)
    copies[-1].wait()
    rows = rows_ref[...]
    unit = rows * lax.rsqrt(jnp.sum(rows * rows, axis=1, keepdims=True) + EPS)
    high, rest = parts_of(unit)
    placed = jnp.dot(
        jnp.concatenate([chosen, chosen], axis=1),
        jnp.concatenate([high, rest.astype(jnp.bfloat16)], axis=0),
        preferred_element_type=jnp.float32,
    )
    for chunk in range(chunks):
        out_ref[pl.ds(chunk, slots, stride=chunks), :] = placed[
            :, chunk * LANES : (chunk + 1) * LANES
        ]
    for copy in copies[1:-1]:
        copy.wait()


def split_rows(rows_ref, high_ref, low_ref, send_cap):
    count, width = high_ref.shape
    chunks = width // LANES
    each = count // send_cap
    for rank in range(send_cap):
        for chunk in range(chunks):
            part = rows_ref[pl.ds(rank * chunks + chunk, each, stride=send_cap * chunks), :]
            high, rest = parts_of(part)
            cols = slice(chunk * LANES, (chunk + 1) * LANES)
            high_ref[rank * each : (rank + 1) * each, cols] = high
            low_ref[rank * each : (rank + 1) * each, cols] = rest.astype(jnp.bfloat16)


def across_lanes(column):
    wide = jnp.broadcast_to(column, (column.shape[0], LANES))
    return wide.T[:1, :]


def masked_max(scores, key_code, query_code, cap):
    first = query_code // cap * cap
    allowed = (key_code < query_code) & (key_code >= first)
    return jnp.max(jnp.where(allowed, scores, -1.0), axis=0, keepdims=True)


def best_of(key_high, key_low, high_turned, low_turned, key_code, query_code, cap):
    def dot(keys, queries):
        return jnp.dot(keys, queries, preferred_element_type=jnp.float32)

    scores = dot(key_high, high_turned) + (
        dot(key_high, low_turned) + dot(key_low, high_turned)
    )
    return masked_max(scores, key_code, query_code, cap)


def near_kernel(send_cap, lists_ref, counts_ref, own_ref, high_ref, low_ref, best_ref,
                other_code_ref, query_code_ref, own_high, own_low):
    slots = own_high.shape[0]
    cap = lists_ref.shape[1]
    core = lax.axis_index("tiles").astype(jnp.int32)
    lists, counts = lists_ref[...], counts_ref[...]
    own_code = codes_of(lists, counts, core, slots, send_cap)
    query_code = across_lanes(own_code)
    query_code_ref[...] = query_code
    other_code_ref[...] = codes_of(lists, counts, 1 - core, slots, send_cap)
    split_rows(own_ref, own_high, own_low, send_cap)
    high, low = own_high[...], own_low[...]
    high_ref[...] = high.T
    low_ref[...] = low.T
    best_ref[...] = best_of(
        high, low, high_ref[...], low_ref[...], own_code, query_code, cap
    )


def far_kernel(send_cap, cap, high_ref, low_ref, best_ref, other_code_ref, query_code_ref,
               other_ref, out_ref):
    width, rows = high_ref.shape
    each = rows // send_cap
    chunks = width // LANES
    step = 2
    scores = jnp.zeros((rows, rows), jnp.float32)
    for begin in range(0, chunks, step):
        part = jnp.concatenate(
            [
                jnp.concatenate(
                    [
                        other_ref[pl.ds(rank * chunks + chunk, each, stride=send_cap * chunks), :]
                        for rank in range(send_cap)
                    ],
                    axis=0,
                )
                for chunk in range(begin, begin + step)
            ],
            axis=1,
        )
        high, rest = parts_of(part)
        low = rest.astype(jnp.bfloat16)
        span = slice(begin * LANES, (begin + step) * LANES)
        high_turned, low_turned = high_ref[span, :], low_ref[span, :]
        scores += (
            jnp.dot(high, high_turned, preferred_element_type=jnp.float32)
            + jnp.dot(high, low_turned, preferred_element_type=jnp.float32)
            + jnp.dot(low, high_turned, preferred_element_type=jnp.float32)
        )
    best = jnp.maximum(
        best_ref[...], masked_max(scores, other_code_ref[...], query_code_ref[...], cap)
    )
    lane = lax.broadcasted_iota(jnp.int32, (each, LANES), 1)
    out = jnp.zeros((each, LANES), jnp.float32)
    for rank in range(send_cap):
        column = jnp.broadcast_to(best[:, rank * each : (rank + 1) * each], (LANES, each)).T
        out = jnp.where(lane == rank, column, out)
    out_ref[...] = out


def pick_kernel(send_cap, slot_ref, back_ref, out_ref):
    homes = back_ref.shape[0]
    docs = slot_ref.shape[1]
    slot = slot_ref[...]
    home = lax.broadcasted_iota(jnp.int32, (homes, docs), 0)
    back = back_ref[...]
    picked = jnp.zeros((homes, docs), jnp.float32)
    for rank in range(send_cap):
        value = jnp.broadcast_to(back[:, rank : rank + 1], (homes, docs))
        picked = jnp.where(slot == home * send_cap + rank, value, picked)
    out_ref[...] = jnp.sum(picked, axis=0, keepdims=True)


def local(embeddings, cluster_of, row_lists, row_counts):
    n_docs = lax.axis_size("docs")
    n_tiles = lax.axis_size("tiles")
    doc_count, width = embeddings.shape
    send_cap = n_tiles * doc_count // n_docs
    cl_local = row_lists.shape[0]
    slots = n_docs * send_cap
    flat = (slots * width // LANES, LANES)
    vmem = pl.BlockSpec(memory_space=pltpu.VMEM)

    hbm = pl.BlockSpec(memory_space=pltpu.HBM)

    def in_hbm(array):
        return pltpu.with_memory_space_constraint(array, pltpu.HBM)

    outgoing, slot, lists, counts = pl.pallas_call(
        functools.partial(prep_kernel, cl_local, send_cap),
        out_shape=(
            jax.ShapeDtypeStruct(flat, jnp.float32),
            jax.ShapeDtypeStruct((1, doc_count), jnp.int32),
            jax.ShapeDtypeStruct(row_lists.shape, jnp.int32),
            jax.ShapeDtypeStruct((1, cl_local), jnp.int32),
        ),
        in_specs=[hbm] * 4,
        out_specs=(vmem,) * 4,
        scratch_shapes=[
            pltpu.VMEM((1, doc_count), jnp.int32),
            pltpu.VMEM((doc_count, width), jnp.float32),
            pltpu.SemaphoreType.DMA((4,)),
        ],
        compiler_params=PARAMS,
        name="prep",
    )(
        in_hbm(cluster_of.reshape(1, doc_count)),
        in_hbm(row_lists),
        in_hbm(row_counts.reshape(1, cl_local)),
        in_hbm(embeddings),
    )

    def exchange(blocks):
        return lax.all_to_all(
            blocks, "docs", split_axis=0, concat_axis=0, tiled=True,
            axis_index_groups=[[regroup(index) for index in range(n_docs)]],
        )

    own = exchange(outgoing.reshape(n_docs, -1, LANES)).reshape(flat)
    other = lax.ppermute(own, "tiles", [(0, 1), (1, 0)])

    cap = row_lists.shape[1]
    turned = jax.ShapeDtypeStruct((width, slots), jnp.bfloat16)
    parts = [pltpu.VMEM((slots, width), jnp.bfloat16)] * 2
    near = pl.pallas_call(
        functools.partial(near_kernel, send_cap),
        out_shape=(
            turned,
            turned,
            jax.ShapeDtypeStruct((1, slots), jnp.float32),
            jax.ShapeDtypeStruct((slots, 1), jnp.int32),
            jax.ShapeDtypeStruct((1, slots), jnp.int32),
        ),
        in_specs=[vmem] * 3,
        out_specs=(vmem,) * 5,
        scratch_shapes=parts,
        compiler_params=PARAMS,
        name="near",
    )(lists, counts, own)
    best = pl.pallas_call(
        functools.partial(far_kernel, send_cap, cap),
        out_shape=jax.ShapeDtypeStruct((n_docs, LANES), jnp.float32),
        in_specs=[vmem] * 6,
        out_specs=vmem,
        compiler_params=PARAMS,
        name="far",
    )(*near, other)

    back = exchange(best.reshape(n_docs, 1, LANES)).reshape(n_docs, LANES)
    picked = pl.pallas_call(
        functools.partial(pick_kernel, send_cap),
        out_shape=jax.ShapeDtypeStruct((1, doc_count), jnp.float32),
        in_specs=[vmem, vmem],
        out_specs=vmem,
        compiler_params=PARAMS,
        name="pick",
    )(slot, back)
    return picked.reshape(doc_count)


def solution(mesh):
    placed = (P(("docs", "tiles"), None), P(("docs", "tiles")), P("docs", None), P("docs"))
    return jax.shard_map(
        local, mesh=mesh, in_specs=placed, out_specs=P(("docs", "tiles")), check_vma=False
    )
```

time: 64.5 us -> 63.6 us (0.986)
  Pallas kernels: 5.61 us -> 4.38 us
  waiting for transfers between devices: 0.01 us -> 0.97 us
  local copies, waits for them, and re-layouts: 0.66 us -> 0 us
    ppermute x1, waiting for transfers between devices: 0.01 us -> 0.97 us  [local(): other = lax.ppermute(own, 'tiles', [(0, 1), (1, 0)])]
    pallas_call x2, Pallas kernels: 3.01 us -> 2.2 us  [the longest x1 1.32 us: local(): pl.pallas_call(functools.partial(near_kernel, send_cap), out_shape=(turne...]
    unnamed x4 -> x0, local copies, waits for them, and re-layouts: 0.66 us -> none
  transfers between devices with their start and end apart: 1 -> 1, of which waited for: 0 -> 1; matrix products, arithmetic and copies ran while one was open for 0% -> 0% of each run, Pallas kernels for 3% -> 2%
where the time goes in v3:
time: 63.6 us; the launch traced here: 63.4 us
  blocking collectives  56.8 us (89%)
  Pallas kernels  4.38 us (7%)
  starting transfers between devices  1.25 us (2%)
  waiting for transfers between devices  0.97 us (2%)
    all_to_all x2, blocking collectives, exchange(): lax.all_to_all(blocks, 'docs', split_axis=0, concat_axis=0, tiled=True, a...  56.8 us
    pallas_call x1, Pallas kernels, local(): pl.pallas_call(functools.partial(prep_kernel, cl_local, send_cap), out_sh...  1.57 us
    pallas_call x1, Pallas kernels, local(): pl.pallas_call(functools.partial(near_kernel, send_cap), out_shape=(turne...  1.32 us
  transfers between devices with their start and end apart: 1, of which 1 were waited for; matrix products, arithmetic and copies ran while one was open for 0% of the time, Pallas kernels for 2%

profile of v3, /device:TPU:1, one launch (start us, length us, event | category | flops | bytes accessed | tf_op | source)
XLA Modules:
  0.0 63.4 jit_solution(738565344186330966)
XLA Ops:
  0.0 1.6 %prep.1 = (f32[2048,128]{1,0:T(8,128)S(1)}, s32[1,128]{1,0:T(1,128)S(1)}, s32[2,512]{1,0:T(2,128)S(1)}, s32[1,2]{1,0:T(1,128)S(1)}) custom-call(s32[1,128]{1,0:T(1,128)} %bitcast.14, s32[2,512]{1,0:T(2,128)} %lists_hbm.1, s32[1,2]{1,0:T(1,128)} %bitcast.15, f32[128,1024]{1,0:T(8,128)} %rows_hbm.1), custom_call_target="tpu_custom_call" | custom-call | tf_op jit(solution)/shard_map/prep/pallas_call | solution.py:209
  1.6 41.0 %all_to_all.10 = f32[128,16,128]{2,1,0:T(8,128)S(1)} all-to-all(f32[128,16,128]{2,1,0:T(8,128)S(1)} %bitcast.11), channel_id=1, replica_groups={{148,150,144,146,156,158,152,154,132,134,128,130,140,142,136,138,180,18..., dimensions={0} | all-to-all | bytes 2097152 | tf_op jit(solution)/shard_map/all_to_all | solution.py:234
  42.6 1.3 %collective-permute-start = (f32[2048,128]{1,0:T(8,128)S(1)}, f32[2048,128]{1,0:T(8,128)S(1)}, u32[]{:S(2)}, u32[]{:S(2)}) collective-permute-start(f32[2048,128]{1,0:T(8,128)S(1)} %bitcast.9), channel_id=1, source_target_pairs={{0,1},{1,0},{2,3},{3,2},{4,5},{5,4},{6,7},{7,6},{8,9},{9,8},{10,11... | collective-permute-start | bytes 3145736 | tf_op jit(solution)/shard_map/ppermute | solution.py:240
  43.8 1.3 %near.1 = (bf16[1024,256]{1,0:T(8,128)(2,1)S(1)}, bf16[1024,256]{1,0:T(8,128)(2,1)S(1)}, f32[1,256]{1,0:T(1,128)S(1)}, s32[256,1]{1,0:T(8,128)S(1)}, s32[1,256]{1,0:T(1,128)S(1)}) custom-call(s32[2,512]{1,0:T(2,128)S(1)} %get-tuple-element.15.lists_ref, s32[1,2]{1,0:T(1,128)S(1)} %get-tuple-element.16.counts_ref, f32[2048,128]{1,0:T(8,128)S(1)} %bitcast.10), custom_call_target="tpu_custom_call" | custom-call | tf_op jit(solution)/shard_map/near/pallas_call | solution.py:245
  45.1 1.0 %collective-permute-done.other_ref = f32[2048,128]{1,0:T(8,128)S(1)} collective-permute-done((f32[2048,128]{1,0:T(8,128)S(1)}, f32[2048,128]{1,0:T(8,128)S(1)}, u32[]{:S(2)}, u32[]{:S(2)}) %collective-permute-start) | collective-permute-done | bytes 1048608 | tf_op jit(solution)/shard_map/ppermute | solution.py:240
  46.1 0.9 %far.1 = f32[128,128]{1,0:T(8,128)S(1)} custom-call(bf16[1024,256]{1,0:T(8,128)(2,1)S(1)} %get-tuple-element.18.high_ref, bf16[1024,256]{1,0:T(8,128)(2,1)S(1)} %get-tuple-element.19.low_ref, f32[1,256]{1,0:T(1,128)S(1)} %get-tuple-element.20.best_ref, s32[256,1]{1,0:T(8,128)S(1)} %get-tuple-element.21.other_code_ref, ...), custom_call_target="tpu_custom_call" | custom-call | tf_op jit(solution)/shard_map/far/pallas_call | solution.py:260
  47.0 15.8 %all_to_all.11 = f32[128,1,128]{2,1,0:T(1,128)S(1)} all-to-all(f32[128,1,128]{2,1,0:T(1,128)S(1)} %bitcast.13), channel_id=1, replica_groups={{148,150,144,146,156,158,152,154,132,134,128,130,140,142,136,138,180,18..., dimensions={0} | all-to-all | bytes 131072 | tf_op jit(solution)/shard_map/all_to_all | solution.py:234
  62.8 0.6 pick.1
Async XLA Ops:
  42.6 3.5 %collective-permute-start = (f32[2048,128]{1,0:T(8,128)S(1)}, f32[2048,128]{1,0:T(8,128)S(1)}, u32[]{:S(2)}, u32[]{:S(2)}) collective-permute-start(f32[2048,128]{1,0:T(8,128)S(1)} %bitcast.9), channel_id=1, source_target_pairs={{0,1},{1,0},{2,3},{3,2},{4,5},{5,4},{6,7},{7,6},{8,9},{9,8},{10,11... | collective-permute-start | bytes 3145736 | tf_op jit(solution)/shard_map/ppermute | solution.py:240

commit v4 on v3

--- a/solution.py
+++ b/solution.py
@@ -2,6 +2,7 @@
 
 import jax
 import jax.numpy as jnp
+import numpy as np
 from jax import lax
 from jax.experimental import pallas as pl
 from jax.experimental.pallas import tpu as pltpu
@@ -9,12 +10,22 @@
 
 EPS = 1e-06
 LANES = 128
-FIRST = 74
+GRID = (8, 4, 4)
 PARAMS = pltpu.CompilerParams(vmem_limit_bytes=32 * 1024 * 1024)
 
 
-def regroup(index):
-    return index ^ FIRST
+def group_order():
+    spots = [
+        (z, x, y) for z in range(GRID[0]) for x in range(GRID[1]) for y in range(GRID[2])
+    ]
+
+    def distance(spot):
+        gaps = [abs(at - size // 2) for at, size in zip(spot, GRID)]
+        return sum(min(gap, size - gap) for gap, size in zip(gaps, GRID))
+
+    return sorted(
+        range(len(spots)), key=lambda index: (distance(spots[index]) > 0, -distance(spots[index]))
+    )
 
 
 def parts_of(rows):
@@ -23,12 +34,10 @@
     return high, rest
 
 
-def codes_of(lists, counts, half, rows, send_cap):
+def codes_of(lists, counts, half, key):
     cap = lists.shape[1]
-    each = rows // send_cap
-    row = lax.broadcasted_iota(jnp.int32, (rows, 1), 0)
-    rank = row // each
-    place = half * rows + regroup(row - rank * each) * send_cap + rank
+    rows = key.shape[0]
+    place = half * rows + key
     position = lax.broadcasted_iota(jnp.int32, (1, cap), 1)
     code = jnp.full((rows, cap), -1, jnp.int32)
     for cluster in range(lists.shape[0]):
@@ -38,8 +47,9 @@
     return jnp.max(code, axis=1, keepdims=True)
 
 
-def prep_kernel(cl_local, send_cap, cluster_hbm, lists_hbm, counts_hbm, rows_hbm,
-                out_ref, slot_ref, lists_ref, counts_ref, cluster_ref, rows_ref, sems):
+def prep_kernel(cl_local, send_cap, table_hbm, cluster_hbm, lists_hbm, counts_hbm, rows_hbm,
+                out_ref, slot_ref, table_ref, lists_ref, counts_ref,
+                cluster_ref, rows_ref, sems):
     docs, width = rows_ref.shape
     slots = out_ref.shape[0] * LANES // width
     chunks = width // LANES
@@ -48,6 +58,7 @@
         for index, (source, target) in enumerate(
             (
                 (cluster_hbm, cluster_ref),
+                (table_hbm, table_ref),
                 (lists_hbm, lists_ref),
                 (counts_hbm, counts_ref),
                 (rows_hbm, rows_ref),
@@ -56,17 +67,27 @@
     ]
     for copy in copies:
         copy.start()
-    copies[0].wait()
+    for copy in copies[:2]:
+        copy.wait()
     home = lax.shift_right_logical(cluster_ref[...], cl_local.bit_length() - 1)
     across = jnp.broadcast_to(home, (docs, docs))
     down = across.T
     sub = lax.broadcasted_iota(jnp.int32, (docs, docs), 0)
     lane = lax.broadcasted_iota(jnp.int32, (docs, docs), 1)
     before = jnp.where((across == down) & (sub < lane), 1, 0)
-    slot = regroup(home) * send_cap + jnp.sum(before, axis=0, keepdims=True)
-    slot_ref[...] = slot
+    rank = jnp.sum(before, axis=0, keepdims=True)
+    slot_ref[...] = home * send_cap + rank
+    homes = slots // send_cap
+    named = lax.broadcasted_iota(jnp.int32, (homes, docs), 0) == home
+    blocks = jnp.broadcast_to(table_ref[1:, :homes].astype(jnp.float32), (8, homes))
+    block = jnp.dot(
+        blocks.astype(jnp.bfloat16),
+        jnp.where(named, 1.0, 0.0).astype(jnp.bfloat16),
+        preferred_element_type=jnp.float32,
+    )[:1].astype(jnp.int32)
     place = lax.broadcasted_iota(jnp.int32, (slots, docs), 0)
-    chosen = jnp.where(place == slot, 1.0, 0.0).astype(jnp.bfloat16)
+    chosen = place == block * send_cap + rank
+    chosen = jnp.where(chosen, 1.0, 0.0).astype(jnp.bfloat16)
     copies[-1].wait()
     rows = rows_ref[...]
     unit = rows * lax.rsqrt(jnp.sum(rows * rows, axis=1, keepdims=True) + EPS)
@@ -80,7 +101,7 @@
         out_ref[pl.ds(chunk, slots, stride=chunks), :] = placed[
             :, chunk * LANES : (chunk + 1) * LANES
         ]
-    for copy in copies[1:-1]:
+    for copy in copies[2:-1]:
         copy.wait()
 
 
@@ -118,16 +139,17 @@
     return masked_max(scores, key_code, query_code, cap)
 
 
-def near_kernel(send_cap, lists_ref, counts_ref, own_ref, high_ref, low_ref, best_ref,
-                other_code_ref, query_code_ref, own_high, own_low):
-    slots = own_high.shape[0]
+def near_kernel(send_cap, table_ref, lists_ref, counts_ref, own_ref, high_ref, low_ref, best_ref,
+                other_code_ref, query_code_ref, key_ref, own_high, own_low):
     cap = lists_ref.shape[1]
+    key = jnp.broadcast_to(table_ref[:1], (LANES, table_ref.shape[1])).T[:, :1]
+    key_ref[...] = key
     core = lax.axis_index("tiles").astype(jnp.int32)
     lists, counts = lists_ref[...], counts_ref[...]
-    own_code = codes_of(lists, counts, core, slots, send_cap)
+    own_code = codes_of(lists, counts, core, key)
     query_code = across_lanes(own_code)
     query_code_ref[...] = query_code
-    other_code_ref[...] = codes_of(lists, counts, 1 - core, slots, send_cap)
+    other_code_ref[...] = codes_of(lists, counts, 1 - core, key)
     split_rows(own_ref, own_high, own_low, send_cap)
     high, low = own_high[...], own_low[...]
     high_ref[...] = high.T
@@ -178,16 +200,14 @@
     out_ref[...] = out
 
 
-def pick_kernel(send_cap, slot_ref, back_ref, out_ref):
+def pick_kernel(send_cap, slot_ref, key_ref, back_ref, out_ref):
     homes = back_ref.shape[0]
     docs = slot_ref.shape[1]
-    slot = slot_ref[...]
-    home = lax.broadcasted_iota(jnp.int32, (homes, docs), 0)
-    back = back_ref[...]
+    slot, key, back = slot_ref[...], key_ref[...], back_ref[...]
     picked = jnp.zeros((homes, docs), jnp.float32)
     for rank in range(send_cap):
         value = jnp.broadcast_to(back[:, rank : rank + 1], (homes, docs))
-        picked = jnp.where(slot == home * send_cap + rank, value, picked)
+        picked = jnp.where(slot == key[rank * homes : (rank + 1) * homes], value, picked)
     out_ref[...] = jnp.sum(picked, axis=0, keepdims=True)
 
 
@@ -206,24 +226,30 @@
     def in_hbm(array):
         return pltpu.with_memory_space_constraint(array, pltpu.HBM)
 
-    outgoing, slot, lists, counts = pl.pallas_call(
+    order = group_order()
+    table = np.zeros((2, slots), np.int32)
+    table[0] = [home * send_cap + rank for rank in range(send_cap) for home in order]
+    table[1, order] = range(n_docs)
+    outgoing, slot, blocks, lists, counts = pl.pallas_call(
         functools.partial(prep_kernel, cl_local, send_cap),
         out_shape=(
             jax.ShapeDtypeStruct(flat, jnp.float32),
             jax.ShapeDtypeStruct((1, doc_count), jnp.int32),
+            jax.ShapeDtypeStruct(table.shape, jnp.int32),
             jax.ShapeDtypeStruct(row_lists.shape, jnp.int32),
             jax.ShapeDtypeStruct((1, cl_local), jnp.int32),
         ),
-        in_specs=[hbm] * 4,
-        out_specs=(vmem,) * 4,
+        in_specs=[hbm] * 5,
+        out_specs=(vmem,) * 5,
         scratch_shapes=[
             pltpu.VMEM((1, doc_count), jnp.int32),
             pltpu.VMEM((doc_count, width), jnp.float32),
-            pltpu.SemaphoreType.DMA((4,)),
+            pltpu.SemaphoreType.DMA((5,)),
         ],
         compiler_params=PARAMS,
         name="prep",
     )(
+        in_hbm(jnp.asarray(table)),
         in_hbm(cluster_of.reshape(1, doc_count)),
         in_hbm(row_lists),
         in_hbm(row_counts.reshape(1, cl_local)),
@@ -233,7 +259,7 @@
     def exchange(blocks):
         return lax.all_to_all(
             blocks, "docs", split_axis=0, concat_axis=0, tiled=True,
-            axis_index_groups=[[regroup(index) for index in range(n_docs)]],
+            axis_index_groups=[order],
         )
 
     own = exchange(outgoing.reshape(n_docs, -1, LANES)).reshape(flat)
@@ -242,7 +268,7 @@
     cap = row_lists.shape[1]
     turned = jax.ShapeDtypeStruct((width, slots), jnp.bfloat16)
     parts = [pltpu.VMEM((slots, width), jnp.bfloat16)] * 2
-    near = pl.pallas_call(
+    *near, key = pl.pallas_call(
         functools.partial(near_kernel, send_cap),
         out_shape=(
             turned,
@@ -250,13 +276,14 @@
             jax.ShapeDtypeStruct((1, slots), jnp.float32),
             jax.ShapeDtypeStruct((slots, 1), jnp.int32),
             jax.ShapeDtypeStruct((1, slots), jnp.int32),
+            jax.ShapeDtypeStruct((slots, 1), jnp.int32),
         ),
-        in_specs=[vmem] * 3,
-        out_specs=(vmem,) * 5,
+        in_specs=[vmem] * 4,
+        out_specs=(vmem,) * 6,
         scratch_shapes=parts,
         compiler_params=PARAMS,
         name="near",
-    )(lists, counts, own)
+    )(blocks, lists, counts, own)
     best = pl.pallas_call(
         functools.partial(far_kernel, send_cap, cap),
         out_shape=jax.ShapeDtypeStruct((n_docs, LANES), jnp.float32),
@@ -270,11 +297,11 @@
     picked = pl.pallas_call(
         functools.partial(pick_kernel, send_cap),
         out_shape=jax.ShapeDtypeStruct((1, doc_count), jnp.float32),
-        in_specs=[vmem, vmem],
+        in_specs=[vmem] * 3,
         out_specs=vmem,
         compiler_params=PARAMS,
         name="pick",
-    )(slot, back)
+    )(slot, key, back)
     return picked.reshape(doc_count)
 
 

time: 63.6 us -> 63.2 us (level)
  no operation moved by 1% of the time
where the time goes in v4:
time: 63.2 us; the launch traced here: 63 us
  blocking collectives  56.3 us (89%)
  Pallas kernels  4.6 us (7%)
  starting transfers between devices  1.19 us (2%)
  waiting for transfers between devices  0.83 us (1%)
    all_to_all x2, blocking collectives, exchange(): lax.all_to_all(blocks, 'docs', split_axis=0, concat_axis=0, tiled=True, a...  56.3 us
    pallas_call x1, Pallas kernels, local(): pl.pallas_call(functools.partial(prep_kernel, cl_local, send_cap), out_sh...  1.6 us
    pallas_call x1, Pallas kernels, local(): pl.pallas_call(functools.partial(near_kernel, send_cap), out_shape=(turne...  1.46 us
  transfers between devices with their start and end apart: 1, of which 1 were waited for; matrix products, arithmetic and copies ran while one was open for 0% of the time, Pallas kernels for 2%

profile of v4, /device:TPU:1, one launch (start us, length us, event | category | flops | bytes accessed | tf_op | source)
XLA Modules:
  0.0 63.0 jit_solution(3894118100723651772)
XLA Ops:
  0.0 1.6 %prep.1 = (f32[2048,128]{1,0:T(8,128)S(1)}, s32[1,128]{1,0:T(1,128)S(1)}, s32[2,256]{1,0:T(2,128)S(1)}, s32[2,512]{1,0:T(2,128)S(1)}, s32[1,2]{1,0:T(1,128)S(1)}) custom-call(s32[2,256]{1,0:T(2,128)} %constant.2.clone.table_hbm, s32[1,128]{1,0:T(1,128)} %bitcast.14, s32[2,512]{1,0:T(2,128)} %lists_hbm.1, s32[1,2]{1,0:T(1,128)} %bitcast.15, f32[128,1024]{1,0:T(8,128)} %rows_hbm.1), custom_call_target="tpu_custom_call" | custom-call | tf_op jit(solution)/shard_map/prep/pallas_call | solution.py:233
  1.6 41.1 %all_to_all.10 = f32[128,16,128]{2,1,0:T(8,128)S(1)} all-to-all(f32[128,16,128]{2,1,0:T(8,128)S(1)} %bitcast.11), channel_id=1, replica_groups={{148,0,2,6,8,24,32,224,4,10,14,16,26,30,34,38,40,56,64,192,226,230,232,..., dimensions={0} | all-to-all | bytes 2097152 | tf_op jit(solution)/shard_map/all_to_all | solution.py:260
  42.7 1.2 %collective-permute-start = (f32[2048,128]{1,0:T(8,128)S(1)}, f32[2048,128]{1,0:T(8,128)S(1)}, u32[]{:S(2)}, u32[]{:S(2)}) collective-permute-start(f32[2048,128]{1,0:T(8,128)S(1)} %bitcast.9), channel_id=1, source_target_pairs={{0,1},{1,0},{2,3},{3,2},{4,5},{5,4},{6,7},{7,6},{8,9},{9,8},{10,11... | collective-permute-start | bytes 3145736 | tf_op jit(solution)/shard_map/ppermute | solution.py:266
  43.9 1.5 %near.1 = (bf16[1024,256]{1,0:T(8,128)(2,1)S(1)}, bf16[1024,256]{1,0:T(8,128)(2,1)S(1)}, f32[1,256]{1,0:T(1,128)S(1)}, s32[256,1]{1,0:T(8,128)S(1)}, s32[1,256]{1,0:T(1,128)S(1)}, /*index=5*/s32[256,1]{1,0:T(8,128)S(1)}) custom-call(s32[2,256]{1,0:T(2,128)S(1)} %get-tuple-element.17.table_ref, s32[2,512]{1,0:T(2,128)S(1)} %get-tuple-element.18.lists_ref, ...), custom_call_target="tpu_custom_call" | custom-call | tf_op jit(solution)/shard_map/near/pallas_call | solution.py:271
  45.4 0.8 %collective-permute-done.other_ref = f32[2048,128]{1,0:T(8,128)S(1)} collective-permute-done((f32[2048,128]{1,0:T(8,128)S(1)}, f32[2048,128]{1,0:T(8,128)S(1)}, u32[]{:S(2)}, u32[]{:S(2)}) %collective-permute-start) | collective-permute-done | bytes 1048608 | tf_op jit(solution)/shard_map/ppermute | solution.py:266
  46.2 0.9 %far.1 = f32[128,128]{1,0:T(8,128)S(1)} custom-call(bf16[1024,256]{1,0:T(8,128)(2,1)S(1)} %get-tuple-element.22.high_ref, bf16[1024,256]{1,0:T(8,128)(2,1)S(1)} %get-tuple-element.23.low_ref, f32[1,256]{1,0:T(1,128)S(1)} %get-tuple-element.24.best_ref, s32[256,1]{1,0:T(8,128)S(1)} %get-tuple-element.25.other_code_ref, ...), custom_call_target="tpu_custom_call" | custom-call | tf_op jit(solution)/shard_map/far/pallas_call | solution.py:287
  47.1 15.2 %all_to_all.11 = f32[128,1,128]{2,1,0:T(1,128)S(1)} all-to-all(f32[128,1,128]{2,1,0:T(1,128)S(1)} %bitcast.13), channel_id=1, replica_groups={{148,0,2,6,8,24,32,224,4,10,14,16,26,30,34,38,40,56,64,192,226,230,232,..., dimensions={0} | all-to-all | bytes 131072 | tf_op jit(solution)/shard_map/all_to_all | solution.py:260
  62.3 0.7 %pick.1 = f32[1,128]{1,0:T(1,128)} custom-call(s32[1,128]{1,0:T(1,128)S(1)} %get-tuple-element.16.slot_ref, s32[256,1]{1,0:T(8,128)S(1)} %get-tuple-element.21.key_ref, f32[128,128]{1,0:T(8,128)S(1)} %bitcast.12), custom_call_target="tpu_custom_call" | custom-call | tf_op jit(solution)/shard_map/pick/pallas_call | solution.py:297
Async XLA Ops:
  42.7 3.5 %collective-permute-start = (f32[2048,128]{1,0:T(8,128)S(1)}, f32[2048,128]{1,0:T(8,128)S(1)}, u32[]{:S(2)}, u32[]{:S(2)}) collective-permute-start(f32[2048,128]{1,0:T(8,128)S(1)} %bitcast.9), channel_id=1, source_target_pairs={{0,1},{1,0},{2,3},{3,2},{4,5},{5,4},{6,7},{7,6},{8,9},{9,8},{10,11... | collective-permute-start | bytes 3145736 | tf_op jit(solution)/shard_map/ppermute | solution.py:266

commit v5 on v4

--- a/solution.py
+++ b/solution.py
@@ -14,13 +14,14 @@
 PARAMS = pltpu.CompilerParams(vmem_limit_bytes=32 * 1024 * 1024)
 
 
-def group_order():
+def group_order(ahead):
     spots = [
         (z, x, y) for z in range(GRID[0]) for x in range(GRID[1]) for y in range(GRID[2])
     ]
+    first = (GRID[0] // 2 + ahead, GRID[1] // 2, GRID[2] // 2)
 
     def distance(spot):
-        gaps = [abs(at - size // 2) for at, size in zip(spot, GRID)]
+        gaps = [abs(at - start) for at, start in zip(spot, first)]
         return sum(min(gap, size - gap) for gap, size in zip(gaps, GRID))
 
     return sorted(
@@ -78,8 +79,10 @@
     rank = jnp.sum(before, axis=0, keepdims=True)
     slot_ref[...] = home * send_cap + rank
     homes = slots // send_cap
+    core = lax.axis_index("tiles").astype(jnp.int32)
+    blocks = jnp.where(core == 0, table_ref[3:4, :homes], table_ref[4:5, :homes])
     named = lax.broadcasted_iota(jnp.int32, (homes, docs), 0) == home
-    blocks = jnp.broadcast_to(table_ref[1:, :homes].astype(jnp.float32), (8, homes))
+    blocks = jnp.broadcast_to(blocks.astype(jnp.float32), (8, homes))
     block = jnp.dot(
         blocks.astype(jnp.bfloat16),
         jnp.where(named, 1.0, 0.0).astype(jnp.bfloat16),
@@ -139,21 +142,35 @@
     return masked_max(scores, key_code, query_code, cap)
 
 
+def down_rows(row):
+    return jnp.broadcast_to(row, (LANES, row.shape[1])).T[:, :1]
+
+
+def turned(rows, turn):
+    return lax.dot_general(
+        rows, turn, (((0,), (0,)), ((), ())), preferred_element_type=jnp.float32
+    ).astype(jnp.bfloat16)
+
+
 def near_kernel(send_cap, table_ref, lists_ref, counts_ref, own_ref, high_ref, low_ref, best_ref,
                 other_code_ref, query_code_ref, key_ref, own_high, own_low):
     cap = lists_ref.shape[1]
-    key = jnp.broadcast_to(table_ref[:1], (LANES, table_ref.shape[1])).T[:, :1]
+    core = lax.axis_index("tiles").astype(jnp.int32)
+    back, one, two = (table_ref[row : row + 1] for row in range(3))
+    own = down_rows(jnp.where(core == 0, one, two))
+    other = down_rows(jnp.where(core == 0, two, one))
+    key = down_rows(back)
     key_ref[...] = key
-    core = lax.axis_index("tiles").astype(jnp.int32)
     lists, counts = lists_ref[...], counts_ref[...]
-    own_code = codes_of(lists, counts, core, key)
-    query_code = across_lanes(own_code)
+    own_code = codes_of(lists, counts, core, own)
+    query_code = across_lanes(codes_of(lists, counts, core, key))
     query_code_ref[...] = query_code
-    other_code_ref[...] = codes_of(lists, counts, 1 - core, key)
+    other_code_ref[...] = codes_of(lists, counts, 1 - core, other)
+    turn = jnp.where(own == back, 1.0, 0.0).astype(jnp.bfloat16)
     split_rows(own_ref, own_high, own_low, send_cap)
     high, low = own_high[...], own_low[...]
-    high_ref[...] = high.T
-    low_ref[...] = low.T
+    high_ref[...] = turned(high, turn)
+    low_ref[...] = turned(low, turn)
     best_ref[...] = best_of(
         high, low, high_ref[...], low_ref[...], own_code, query_code, cap
     )
@@ -226,10 +243,13 @@
     def in_hbm(array):
         return pltpu.with_memory_space_constraint(array, pltpu.HBM)
 
-    order = group_order()
-    table = np.zeros((2, slots), np.int32)
-    table[0] = [home * send_cap + rank for rank in range(send_cap) for home in order]
-    table[1, order] = range(n_docs)
+    order = group_order(0)
+    firsts = [group_order(core) for core in range(n_tiles)]
+    table = np.zeros((1 + 2 * n_tiles, slots), np.int32)
+    for row, homes in enumerate([order] + firsts):
+        table[row] = [home * send_cap + rank for rank in range(send_cap) for home in homes]
+    for core, homes in enumerate(firsts):
+        table[1 + n_tiles + core, homes] = range(n_docs)
     outgoing, slot, blocks, lists, counts = pl.pallas_call(
         functools.partial(prep_kernel, cl_local, send_cap),
         out_shape=(
@@ -256,13 +276,14 @@
         in_hbm(embeddings),
     )
 
-    def exchange(blocks):
+    def exchange(blocks, axis, groups):
         return lax.all_to_all(
-            blocks, "docs", split_axis=0, concat_axis=0, tiled=True,
-            axis_index_groups=[order],
+            blocks, axis, split_axis=0, concat_axis=0, tiled=True, axis_index_groups=groups
         )
 
-    own = exchange(outgoing.reshape(n_docs, -1, LANES)).reshape(flat)
+    groups = [[home * n_tiles + core for home in homes] for core, homes in enumerate(firsts)]
+    own = exchange(outgoing.reshape(n_docs, -1, LANES), ("docs", "tiles"), groups)
+    own = own.reshape(flat)
     other = lax.ppermute(own, "tiles", [(0, 1), (1, 0)])
 
     cap = row_lists.shape[1]
@@ -293,7 +314,7 @@
         name="far",
     )(*near, other)
 
-    back = exchange(best.reshape(n_docs, 1, LANES)).reshape(n_docs, LANES)
+    back = exchange(best.reshape(n_docs, 1, LANES), "docs", [order]).reshape(n_docs, LANES)
     picked = pl.pallas_call(
         functools.partial(pick_kernel, send_cap),
         out_shape=jax.ShapeDtypeStruct((1, doc_count), jnp.float32),

time: 63.2 us -> 63 us (level)
  blocking collectives: 56.3 us -> 54.7 us
  starting transfers between devices: 1.19 us -> 2.58 us
    all_to_all x2, blocking collectives: 56.3 us -> 54.7 us  [exchange(): lax.all_to_all(blocks, axis, split_axis=0, concat_axis=0, tiled=True, axi...]
    ppermute x1, starting transfers between devices: 1.19 us -> 2.58 us  [local(): other = lax.ppermute(own, 'tiles', [(0, 1), (1, 0)])]
  transfers between devices with their start and end apart: 1 -> 1, of which waited for: 1 -> 1; matrix products, arithmetic and copies ran while one was open for 0% -> 0% of each run, Pallas kernels for 2% -> 3%
where the time goes in v5:
time: 63 us; the launch traced here: 62.8 us
  blocking collectives  54.7 us (87%)
  Pallas kernels  4.9 us (8%)
  starting transfers between devices  2.58 us (4%)
    all_to_all x2, blocking collectives, exchange(): lax.all_to_all(blocks, axis, split_axis=0, concat_axis=0, tiled=True, axi...  54.7 us
    ppermute x1, starting transfers between devices, local(): other = lax.ppermute(own, 'tiles', [(0, 1), (1, 0)])  2.58 us
    pallas_call x1, Pallas kernels, local(): pl.pallas_call(functools.partial(near_kernel, send_cap), out_shape=(turne...  1.76 us
    pallas_call x1, Pallas kernels, local(): pl.pallas_call(functools.partial(prep_kernel, cl_local, send_cap), out_sh...  1.6 us
  transfers between devices with their start and end apart: 1, of which 1 were waited for; matrix products, arithmetic and copies ran while one was open for 0% of the time, Pallas kernels for 3%

profile of v5, /device:TPU:1, one launch (start us, length us, event | category | flops | bytes accessed | tf_op | source)
XLA Modules:
  0.0 62.8 jit_solution(16949711372219559045)
XLA Ops:
  0.0 1.6 %prep.1 = (f32[2048,128]{1,0:T(8,128)S(1)}, s32[1,128]{1,0:T(1,128)S(1)}, s32[5,256]{1,0:T(8,128)S(1)}, s32[2,512]{1,0:T(2,128)S(1)}, s32[1,2]{1,0:T(1,128)S(1)}) custom-call(s32[5,256]{1,0:T(8,128)} %constant.2.clone.table_hbm, s32[1,128]{1,0:T(1,128)} %bitcast.14, s32[2,512]{1,0:T(2,128)} %lists_hbm.1, s32[1,2]{1,0:T(1,128)} %bitcast.15, f32[128,1024]{1,0:T(8,128)} %rows_hbm.1), custom_call_target="tpu_custom_call" | custom-call | tf_op jit(solution)/shard_map/prep/pallas_call | solution.py:253
  1.6 39.2 %all_to_all.10 = f32[128,16,128]{2,1,0:T(8,128)S(1)} all-to-all(f32[128,16,128]{2,1,0:T(8,128)S(1)} %bitcast.11), channel_id=1, replica_groups={{148,0,2,6,8,24,32,224,4,10,14,16,26,30,34,38,40,56,64,192,226,230,232,..., dimensions={0} | all-to-all | bytes 2097152 | tf_op jit(solution)/shard_map/all_to_all | solution.py:280
  40.8 2.6 %collective-permute-start = (f32[2048,128]{1,0:T(8,128)S(1)}, f32[2048,128]{1,0:T(8,128)S(1)}, u32[]{:S(2)}, u32[]{:S(2)}) collective-permute-start(f32[2048,128]{1,0:T(8,128)S(1)} %bitcast.9), channel_id=1, source_target_pairs={{0,1},{1,0},{2,3},{3,2},{4,5},{5,4},{6,7},{7,6},{8,9},{9,8},{10,11... | collective-permute-start | bytes 3145736 | tf_op jit(solution)/shard_map/ppermute | solution.py:287
  43.4 1.8 %near.1 = (bf16[1024,256]{1,0:T(8,128)(2,1)S(1)}, bf16[1024,256]{1,0:T(8,128)(2,1)S(1)}, f32[1,256]{1,0:T(1,128)S(1)}, s32[256,1]{1,0:T(8,128)S(1)}, s32[1,256]{1,0:T(1,128)S(1)}, /*index=5*/s32[256,1]{1,0:T(8,128)S(1)}) custom-call(s32[5,256]{1,0:T(8,128)S(1)} %get-tuple-element.17.table_ref, s32[2,512]{1,0:T(2,128)S(1)} %get-tuple-element.18.lists_ref, ...), custom_call_target="tpu_custom_call" | custom-call | tf_op jit(solution)/shard_map/near/pallas_call | solution.py:292
  45.1 0.5 collective-permute-done.other_ref
  45.7 0.9 %far.1 = f32[128,128]{1,0:T(8,128)S(1)} custom-call(bf16[1024,256]{1,0:T(8,128)(2,1)S(1)} %get-tuple-element.22.high_ref, bf16[1024,256]{1,0:T(8,128)(2,1)S(1)} %get-tuple-element.23.low_ref, f32[1,256]{1,0:T(1,128)S(1)} %get-tuple-element.24.best_ref, s32[256,1]{1,0:T(8,128)S(1)} %get-tuple-element.25.other_code_ref, ...), custom_call_target="tpu_custom_call" | custom-call | tf_op jit(solution)/shard_map/far/pallas_call | solution.py:308
  46.6 15.5 %all_to_all.11 = f32[128,1,128]{2,1,0:T(1,128)S(1)} all-to-all(f32[128,1,128]{2,1,0:T(1,128)S(1)} %bitcast.13), channel_id=1, replica_groups={{148,0,2,6,8,24,32,224,4,10,14,16,26,30,34,38,40,56,64,192,226,230,232,..., dimensions={0} | all-to-all | bytes 131072 | tf_op jit(solution)/shard_map/all_to_all | solution.py:280
  62.1 0.7 %pick.1 = f32[1,128]{1,0:T(1,128)} custom-call(s32[1,128]{1,0:T(1,128)S(1)} %get-tuple-element.16.slot_ref, s32[256,1]{1,0:T(8,128)S(1)} %get-tuple-element.21.key_ref, f32[128,128]{1,0:T(8,128)S(1)} %bitcast.12), custom_call_target="tpu_custom_call" | custom-call | tf_op jit(solution)/shard_map/pick/pallas_call | solution.py:318
Async XLA Ops:
  40.8 4.9 %collective-permute-start = (f32[2048,128]{1,0:T(8,128)S(1)}, f32[2048,128]{1,0:T(8,128)S(1)}, u32[]{:S(2)}, u32[]{:S(2)}) collective-permute-start(f32[2048,128]{1,0:T(8,128)S(1)} %bitcast.9), channel_id=1, source_target_pairs={{0,1},{1,0},{2,3},{3,2},{4,5},{5,4},{6,7},{7,6},{8,9},{9,8},{10,11... | collective-permute-start | bytes 3145736 | tf_op jit(solution)/shard_map/ppermute | solution.py:287

commit v6 on v5

--- a/solution.py
+++ b/solution.py
@@ -27,6 +27,16 @@
     return sorted(
         range(len(spots)), key=lambda index: (distance(spots[index]) > 0, -distance(spots[index]))
     )
+
+
+def return_order():
+    count = GRID[0] * GRID[1] * GRID[2]
+    bits = count.bit_length() - 1
+    first = group_order(0)[0]
+    return [
+        first ^ sum((index >> bit & 1) << (bits - 1 - bit) for bit in range(bits))
+        for index in range(count)
+    ]
 
 
 def parts_of(rows):
@@ -243,7 +253,7 @@
     def in_hbm(array):
         return pltpu.with_memory_space_constraint(array, pltpu.HBM)
 
-    order = group_order(0)
+    order = return_order()
     firsts = [group_order(core) for core in range(n_tiles)]
     table = np.zeros((1 + 2 * n_tiles, slots), np.int32)
     for row, homes in enumerate([order] + firsts):

time: 63 us -> 62.7 us (level)
  no operation moved by 1% of the time
where the time goes in v6:
time: 62.7 us; the launch traced here: 62.6 us
  blocking collectives  54.5 us (87%)
  Pallas kernels  4.9 us (8%)
  starting transfers between devices  2.58 us (4%)
    all_to_all x2, blocking collectives, exchange(): lax.all_to_all(blocks, axis, split_axis=0, concat_axis=0, tiled=True, axi...  54.5 us
    ppermute x1, starting transfers between devices, local(): other = lax.ppermute(own, 'tiles', [(0, 1), (1, 0)])  2.58 us
    pallas_call x1, Pallas kernels, local(): pl.pallas_call(functools.partial(near_kernel, send_cap), out_shape=(turne...  1.76 us
    pallas_call x1, Pallas kernels, local(): pl.pallas_call(functools.partial(prep_kernel, cl_local, send_cap), out_sh...  1.6 us
  transfers between devices with their start and end apart: 1, of which 1 were waited for; matrix products, arithmetic and copies ran while one was open for 0% of the time, Pallas kernels for 3%

profile of v6, /device:TPU:1, one launch (start us, length us, event | category | flops | bytes accessed | tf_op | source)
XLA Modules:
  0.0 62.6 jit_solution(4728184215151727242)
XLA Ops:
  0.0 1.6 %prep.1 = (f32[2048,128]{1,0:T(8,128)S(1)}, s32[1,128]{1,0:T(1,128)S(1)}, s32[5,256]{1,0:T(8,128)S(1)}, s32[2,512]{1,0:T(2,128)S(1)}, s32[1,2]{1,0:T(1,128)S(1)}) custom-call(s32[5,256]{1,0:T(8,128)} %constant.2.clone.table_hbm, s32[1,128]{1,0:T(1,128)} %bitcast.14, s32[2,512]{1,0:T(2,128)} %lists_hbm.1, s32[1,2]{1,0:T(1,128)} %bitcast.15, f32[128,1024]{1,0:T(8,128)} %rows_hbm.1), custom_call_target="tpu_custom_call" | custom-call | tf_op jit(solution)/shard_map/prep/pallas_call | solution.py:263
  1.6 39.2 %all_to_all.10 = f32[128,16,128]{2,1,0:T(8,128)S(1)} all-to-all(f32[128,16,128]{2,1,0:T(8,128)S(1)} %bitcast.11), channel_id=1, replica_groups={{148,0,2,6,8,24,32,224,4,10,14,16,26,30,34,38,40,56,64,192,226,230,232,..., dimensions={0} | all-to-all | bytes 2097152 | tf_op jit(solution)/shard_map/all_to_all | solution.py:290
  40.8 2.6 %collective-permute-start = (f32[2048,128]{1,0:T(8,128)S(1)}, f32[2048,128]{1,0:T(8,128)S(1)}, u32[]{:S(2)}, u32[]{:S(2)}) collective-permute-start(f32[2048,128]{1,0:T(8,128)S(1)} %bitcast.9), channel_id=1, source_target_pairs={{0,1},{1,0},{2,3},{3,2},{4,5},{5,4},{6,7},{7,6},{8,9},{9,8},{10,11... | collective-permute-start | bytes 3145736 | tf_op jit(solution)/shard_map/ppermute | solution.py:297
  43.4 1.8 %near.1 = (bf16[1024,256]{1,0:T(8,128)(2,1)S(1)}, bf16[1024,256]{1,0:T(8,128)(2,1)S(1)}, f32[1,256]{1,0:T(1,128)S(1)}, s32[256,1]{1,0:T(8,128)S(1)}, s32[1,256]{1,0:T(1,128)S(1)}, /*index=5*/s32[256,1]{1,0:T(8,128)S(1)}) custom-call(s32[5,256]{1,0:T(8,128)S(1)} %get-tuple-element.17.table_ref, s32[2,512]{1,0:T(2,128)S(1)} %get-tuple-element.18.lists_ref, ...), custom_call_target="tpu_custom_call" | custom-call | tf_op jit(solution)/shard_map/near/pallas_call | solution.py:302
  45.1 0.5 collective-permute-done.other_ref
  45.7 0.9 %far.1 = f32[128,128]{1,0:T(8,128)S(1)} custom-call(bf16[1024,256]{1,0:T(8,128)(2,1)S(1)} %get-tuple-element.22.high_ref, bf16[1024,256]{1,0:T(8,128)(2,1)S(1)} %get-tuple-element.23.low_ref, f32[1,256]{1,0:T(1,128)S(1)} %get-tuple-element.24.best_ref, s32[256,1]{1,0:T(8,128)S(1)} %get-tuple-element.25.other_code_ref, ...), custom_call_target="tpu_custom_call" | custom-call | tf_op jit(solution)/shard_map/far/pallas_call | solution.py:318
  46.6 15.3 %all_to_all.11 = f32[128,1,128]{2,1,0:T(1,128)S(1)} all-to-all(f32[128,1,128]{2,1,0:T(1,128)S(1)} %bitcast.13), channel_id=1, replica_groups={{148,20,212,84,180,52,244,116,132,4,196,68,164,36,228,100,156,28,220,92..., dimensions={0} | all-to-all | bytes 131072 | tf_op jit(solution)/shard_map/all_to_all | solution.py:290
  61.9 0.7 %pick.1 = f32[1,128]{1,0:T(1,128)} custom-call(s32[1,128]{1,0:T(1,128)S(1)} %get-tuple-element.16.slot_ref, s32[256,1]{1,0:T(8,128)S(1)} %get-tuple-element.21.key_ref, f32[128,128]{1,0:T(8,128)S(1)} %bitcast.12), custom_call_target="tpu_custom_call" | custom-call | tf_op jit(solution)/shard_map/pick/pallas_call | solution.py:328
Async XLA Ops:
  40.8 4.9 %collective-permute-start = (f32[2048,128]{1,0:T(8,128)S(1)}, f32[2048,128]{1,0:T(8,128)S(1)}, u32[]{:S(2)}, u32[]{:S(2)}) collective-permute-start(f32[2048,128]{1,0:T(8,128)S(1)} %bitcast.9), channel_id=1, source_target_pairs={{0,1},{1,0},{2,3},{3,2},{4,5},{5,4},{6,7},{7,6},{8,9},{9,8},{10,11... | collective-permute-start | bytes 3145736 | tf_op jit(solution)/shard_map/ppermute | solution.py:297

commit v7 on v6

--- a/solution.py
+++ b/solution.py
@@ -153,7 +153,7 @@
 
 
 def down_rows(row):
-    return jnp.broadcast_to(row, (LANES, row.shape[1])).T[:, :1]
+    return jnp.broadcast_to(row, (LANES, row.shape[1])).T
 
 
 def turned(rows, turn):
@@ -167,15 +167,18 @@
     cap = lists_ref.shape[1]
     core = lax.axis_index("tiles").astype(jnp.int32)
     back, one, two = (table_ref[row : row + 1] for row in range(3))
-    own = down_rows(jnp.where(core == 0, one, two))
-    other = down_rows(jnp.where(core == 0, two, one))
-    key = down_rows(back)
-    key_ref[...] = key
+    own = down_rows(jnp.where(core == 0, one, two))[:, :1]
+    other = down_rows(jnp.where(core == 0, two, one))[:, :1]
+    wide = down_rows(back)
+    key_ref[...] = wide
+    key = wide[:, :1]
     lists, counts = lists_ref[...], counts_ref[...]
     own_code = codes_of(lists, counts, core, own)
     query_code = across_lanes(codes_of(lists, counts, core, key))
     query_code_ref[...] = query_code
-    other_code_ref[...] = codes_of(lists, counts, 1 - core, other)
+    other_code_ref[...] = jnp.broadcast_to(
+        codes_of(lists, counts, 1 - core, other), other_code_ref.shape
+    )
     turn = jnp.where(own == back, 1.0, 0.0).astype(jnp.bfloat16)
     split_rows(own_ref, own_high, own_low, send_cap)
     high, low = own_high[...], own_low[...]
@@ -305,9 +308,9 @@
             turned,
             turned,
             jax.ShapeDtypeStruct((1, slots), jnp.float32),
-            jax.ShapeDtypeStruct((slots, 1), jnp.int32),
+            jax.ShapeDtypeStruct((slots, slots), jnp.int32),
             jax.ShapeDtypeStruct((1, slots), jnp.int32),
-            jax.ShapeDtypeStruct((slots, 1), jnp.int32),
+            jax.ShapeDtypeStruct((slots, LANES), jnp.int32),
         ),
         in_specs=[vmem] * 4,
         out_specs=(vmem,) * 6,

time: 62.7 us -> 62.7 us (level)
  no operation moved by 1% of the time
where the time goes in v7:
time: 62.7 us; the launch traced here: 62.5 us
  blocking collectives  54.5 us (87%)
  Pallas kernels  4.87 us (8%)
  starting transfers between devices  2.58 us (4%)
    all_to_all x2, blocking collectives, exchange(): lax.all_to_all(blocks, axis, split_axis=0, concat_axis=0, tiled=True, axi...  54.5 us
    ppermute x1, starting transfers between devices, local(): other = lax.ppermute(own, 'tiles', [(0, 1), (1, 0)])  2.58 us
    pallas_call x1, Pallas kernels, local(): pl.pallas_call(functools.partial(near_kernel, send_cap), out_shape=(turne...  1.76 us
    pallas_call x1, Pallas kernels, local(): pl.pallas_call(functools.partial(prep_kernel, cl_local, send_cap), out_sh...  1.6 us
  transfers between devices with their start and end apart: 1, of which 1 were waited for; matrix products, arithmetic and copies ran while one was open for 0% of the time, Pallas kernels for 3%

profile of v7, /device:TPU:1, one launch (start us, length us, event | category | flops | bytes accessed | tf_op | source)
XLA Modules:
  0.0 62.5 jit_solution(4865776927426906264)
XLA Ops:
  0.0 1.6 %prep.1 = (f32[2048,128]{1,0:T(8,128)S(1)}, s32[1,128]{1,0:T(1,128)S(1)}, s32[5,256]{1,0:T(8,128)S(1)}, s32[2,512]{1,0:T(2,128)S(1)}, s32[1,2]{1,0:T(1,128)S(1)}) custom-call(s32[5,256]{1,0:T(8,128)} %constant.2.clone.table_hbm, s32[1,128]{1,0:T(1,128)} %bitcast.14, s32[2,512]{1,0:T(2,128)} %lists_hbm.1, s32[1,2]{1,0:T(1,128)} %bitcast.15, f32[128,1024]{1,0:T(8,128)} %rows_hbm.1), custom_call_target="tpu_custom_call" | custom-call | tf_op jit(solution)/shard_map/prep/pallas_call | solution.py:266
  1.6 39.2 %all_to_all.10 = f32[128,16,128]{2,1,0:T(8,128)S(1)} all-to-all(f32[128,16,128]{2,1,0:T(8,128)S(1)} %bitcast.11), channel_id=1, replica_groups={{148,0,2,6,8,24,32,224,4,10,14,16,26,30,34,38,40,56,64,192,226,230,232,..., dimensions={0} | all-to-all | bytes 2097152 | tf_op jit(solution)/shard_map/all_to_all | solution.py:293
  40.8 2.6 %collective-permute-start = (f32[2048,128]{1,0:T(8,128)S(1)}, f32[2048,128]{1,0:T(8,128)S(1)}, u32[]{:S(2)}, u32[]{:S(2)}) collective-permute-start(f32[2048,128]{1,0:T(8,128)S(1)} %bitcast.9), channel_id=1, source_target_pairs={{0,1},{1,0},{2,3},{3,2},{4,5},{5,4},{6,7},{7,6},{8,9},{9,8},{10,11... | collective-permute-start | bytes 3145736 | tf_op jit(solution)/shard_map/ppermute | solution.py:300
  43.4 1.8 %near.1 = (bf16[1024,256]{1,0:T(8,128)(2,1)S(1)}, bf16[1024,256]{1,0:T(8,128)(2,1)S(1)}, f32[1,256]{1,0:T(1,128)S(1)}, s32[256,256]{1,0:T(8,128)S(1)}, s32[1,256]{1,0:T(1,128)S(1)}, /*index=5*/s32[256,128]{1,0:T(8,128)S(1)}) custom-call(s32[5,256]{1,0:T(8,128)S(1)} %get-tuple-element.17.table_ref, s32[2,512]{1,0:T(2,128)S(1)} %get-tuple-element.18.lists_ref, ...), custom_call_target="tpu_custom_call" | custom-call | tf_op jit(solution)/shard_map/near/pallas_call | solution.py:305
  45.1 0.5 collective-permute-done.other_ref
  45.7 0.9 %far.1 = f32[128,128]{1,0:T(8,128)S(1)} custom-call(bf16[1024,256]{1,0:T(8,128)(2,1)S(1)} %get-tuple-element.22.high_ref, bf16[1024,256]{1,0:T(8,128)(2,1)S(1)} %get-tuple-element.23.low_ref, f32[1,256]{1,0:T(1,128)S(1)} %get-tuple-element.24.best_ref, s32[256,256]{1,0:T(8,128)S(1)} %get-tuple-element.25.other_code_ref, ...), custom_call_target="tpu_custom_call" | custom-call | tf_op jit(solution)/shard_map/far/pallas_call | solution.py:321
  46.6 15.3 %all_to_all.11 = f32[128,1,128]{2,1,0:T(1,128)S(1)} all-to-all(f32[128,1,128]{2,1,0:T(1,128)S(1)} %bitcast.12), channel_id=1, replica_groups={{148,20,212,84,180,52,244,116,132,4,196,68,164,36,228,100,156,28,220,92..., dimensions={0} | all-to-all | bytes 131072 | tf_op jit(solution)/shard_map/all_to_all | solution.py:293
  61.9 0.6 pick.1
Async XLA Ops:
  40.8 4.9 %collective-permute-start = (f32[2048,128]{1,0:T(8,128)S(1)}, f32[2048,128]{1,0:T(8,128)S(1)}, u32[]{:S(2)}, u32[]{:S(2)}) collective-permute-start(f32[2048,128]{1,0:T(8,128)S(1)} %bitcast.9), channel_id=1, source_target_pairs={{0,1},{1,0},{2,3},{3,2},{4,5},{5,4},{6,7},{7,6},{8,9},{9,8},{10,11... | collective-permute-start | bytes 3145736 | tf_op jit(solution)/shard_map/ppermute | solution.py:300

commit v8 on v7

--- a/solution.py
+++ b/solution.py
@@ -176,9 +176,7 @@
     own_code = codes_of(lists, counts, core, own)
     query_code = across_lanes(codes_of(lists, counts, core, key))
     query_code_ref[...] = query_code
-    other_code_ref[...] = jnp.broadcast_to(
-        codes_of(lists, counts, 1 - core, other), other_code_ref.shape
-    )
+    other_code_ref[...] = codes_of(lists, counts, 1 - core, other)
     turn = jnp.where(own == back, 1.0, 0.0).astype(jnp.bfloat16)
     split_rows(own_ref, own_high, own_low, send_cap)
     high, low = own_high[...], own_low[...]
@@ -308,7 +306,7 @@
             turned,
             turned,
             jax.ShapeDtypeStruct((1, slots), jnp.float32),
-            jax.ShapeDtypeStruct((slots, slots), jnp.int32),
+            jax.ShapeDtypeStruct((slots, 1), jnp.int32),
             jax.ShapeDtypeStruct((1, slots), jnp.int32),
             jax.ShapeDtypeStruct((slots, LANES), jnp.int32),
         ),

time: 62.7 us -> 62.7 us (level)
  no operation moved by 1% of the time
where the time goes in v8:
time: 62.7 us; the launch traced here: 62.5 us
  blocking collectives  54.5 us (87%)
  Pallas kernels  4.87 us (8%)
  starting transfers between devices  2.58 us (4%)
    all_to_all x2, blocking collectives, exchange(): lax.all_to_all(blocks, axis, split_axis=0, concat_axis=0, tiled=True, axi...  54.5 us
    ppermute x1, starting transfers between devices, local(): other = lax.ppermute(own, 'tiles', [(0, 1), (1, 0)])  2.58 us
    pallas_call x1, Pallas kernels, local(): pl.pallas_call(functools.partial(near_kernel, send_cap), out_shape=(turne...  1.76 us
    pallas_call x1, Pallas kernels, local(): pl.pallas_call(functools.partial(prep_kernel, cl_local, send_cap), out_sh...  1.6 us
  transfers between devices with their start and end apart: 1, of which 1 were waited for; matrix products, arithmetic and copies ran while one was open for 0% of the time, Pallas kernels for 3%

profile of v8, /device:TPU:1, one launch (start us, length us, event | category | flops | bytes accessed | tf_op | source)
XLA Modules:
  0.0 62.5 jit_solution(596726242218996986)
XLA Ops:
  0.0 1.6 %prep.1 = (f32[2048,128]{1,0:T(8,128)S(1)}, s32[1,128]{1,0:T(1,128)S(1)}, s32[5,256]{1,0:T(8,128)S(1)}, s32[2,512]{1,0:T(2,128)S(1)}, s32[1,2]{1,0:T(1,128)S(1)}) custom-call(s32[5,256]{1,0:T(8,128)} %constant.2.clone.table_hbm, s32[1,128]{1,0:T(1,128)} %bitcast.14, s32[2,512]{1,0:T(2,128)} %lists_hbm.1, s32[1,2]{1,0:T(1,128)} %bitcast.15, f32[128,1024]{1,0:T(8,128)} %rows_hbm.1), custom_call_target="tpu_custom_call" | custom-call | tf_op jit(solution)/shard_map/prep/pallas_call | solution.py:264
  1.6 39.2 %all_to_all.10 = f32[128,16,128]{2,1,0:T(8,128)S(1)} all-to-all(f32[128,16,128]{2,1,0:T(8,128)S(1)} %bitcast.11), channel_id=1, replica_groups={{148,0,2,6,8,24,32,224,4,10,14,16,26,30,34,38,40,56,64,192,226,230,232,..., dimensions={0} | all-to-all | bytes 2097152 | tf_op jit(solution)/shard_map/all_to_all | solution.py:291
  40.8 2.6 %collective-permute-start = (f32[2048,128]{1,0:T(8,128)S(1)}, f32[2048,128]{1,0:T(8,128)S(1)}, u32[]{:S(2)}, u32[]{:S(2)}) collective-permute-start(f32[2048,128]{1,0:T(8,128)S(1)} %bitcast.9), channel_id=1, source_target_pairs={{0,1},{1,0},{2,3},{3,2},{4,5},{5,4},{6,7},{7,6},{8,9},{9,8},{10,11... | collective-permute-start | bytes 3145736 | tf_op jit(solution)/shard_map/ppermute | solution.py:298
  43.4 1.8 %near.1 = (bf16[1024,256]{1,0:T(8,128)(2,1)S(1)}, bf16[1024,256]{1,0:T(8,128)(2,1)S(1)}, f32[1,256]{1,0:T(1,128)S(1)}, s32[256,1]{1,0:T(8,128)S(1)}, s32[1,256]{1,0:T(1,128)S(1)}, /*index=5*/s32[256,128]{1,0:T(8,128)S(1)}) custom-call(s32[5,256]{1,0:T(8,128)S(1)} %get-tuple-element.17.table_ref, s32[2,512]{1,0:T(2,128)S(1)} %get-tuple-element.18.lists_ref, ...), custom_call_target="tpu_custom_call" | custom-call | tf_op jit(solution)/shard_map/near/pallas_call | solution.py:303
  45.1 0.5 collective-permute-done.other_ref
  45.7 0.9 %far.1 = f32[128,128]{1,0:T(8,128)S(1)} custom-call(bf16[1024,256]{1,0:T(8,128)(2,1)S(1)} %get-tuple-element.22.high_ref, bf16[1024,256]{1,0:T(8,128)(2,1)S(1)} %get-tuple-element.23.low_ref, f32[1,256]{1,0:T(1,128)S(1)} %get-tuple-element.24.best_ref, s32[256,1]{1,0:T(8,128)S(1)} %get-tuple-element.25.other_code_ref, ...), custom_call_target="tpu_custom_call" | custom-call | tf_op jit(solution)/shard_map/far/pallas_call | solution.py:319
  46.6 15.3 %all_to_all.11 = f32[128,1,128]{2,1,0:T(1,128)S(1)} all-to-all(f32[128,1,128]{2,1,0:T(1,128)S(1)} %bitcast.13), channel_id=1, replica_groups={{148,20,212,84,180,52,244,116,132,4,196,68,164,36,228,100,156,28,220,92..., dimensions={0} | all-to-all | bytes 131072 | tf_op jit(solution)/shard_map/all_to_all | solution.py:291
  61.9 0.6 pick.1
Async XLA Ops:
  40.8 4.9 %collective-permute-start = (f32[2048,128]{1,0:T(8,128)S(1)}, f32[2048,128]{1,0:T(8,128)S(1)}, u32[]{:S(2)}, u32[]{:S(2)}) collective-permute-start(f32[2048,128]{1,0:T(8,128)S(1)} %bitcast.9), channel_id=1, source_target_pairs={{0,1},{1,0},{2,3},{3,2},{4,5},{5,4},{6,7},{7,6},{8,9},{9,8},{10,11... | collective-permute-start | bytes 3145736 | tf_op jit(solution)/shard_map/ppermute | solution.py:298
